TPU v7x, 512 devices: a whole 4x4x16 slice. The times are simulated.
512 devices in a mesh: noise: 16 (over z_hi, x, core), dp: 32 (over z_lo, y).
Axes of the slice: x: 4, y: 4, z: 16 (z_hi: 2, z_lo: 8; z = z_hi * 8 + z_lo), core: 2. Of those that a mesh axis runs over, the one named last changes fastest.
Arguments:
- noise: bfloat16 [1024, 16384], P('noise', 'dp'), may hold values from -6 to 6
- data: bfloat16 [8192, 16384], P('dp', 'noise'), may hold values from -6 to 6
- timestep: int32 [1024], P('noise'), may hold values from 0 to 999
Outputs:
- inputs_t: bfloat16 [1024, 16384], P('noise', 'dp')
- velocity: bfloat16 [1024, 16384], P('noise', 'dp')
All inputs are finite; a program needn't handle non-finite values.
Results may differ from a plain program's by a relative error of at most 0.011.
Values may be sent and summed in bfloat16 or wider, within the bound.
A program may use at most 64 MiB of HBM per device.

v0:
```python
import jax
import jax.numpy as jnp
from jax import lax
from jax.sharding import PartitionSpec as P

ITERS = 4
NBINS = 1000


EPS = 0.002


def row_lse(scores):
    local_peak = jnp.max(scores, axis=1)
    peak = lax.pmax(local_peak, "dp")
    total = lax.psum(jnp.sum(jnp.exp(scores - peak[:, None]), axis=1), "dp")
    return peak + jnp.log(total)


def col_lse(scores):
    local_peak = jnp.max(scores, axis=0)
    peak = lax.pmax(local_peak, "noise")
    total = lax.psum(jnp.sum(jnp.exp(scores - peak[None, :]), axis=0), "noise")
    return peak + jnp.log(total)


def per_device(noise, data, timestep):
    data_full = lax.all_gather(data, "noise", axis=1, tiled=True)
    width = data_full.shape[1]
    count_cols = data_full.shape[0]
    sq_data = jnp.einsum("cd,cd->c", data_full, data_full, preferred_element_type=jnp.float32)
    piece = lax.all_gather(noise, "dp", axis=1, tiled=True)
    cross = lax.dot_general(
        piece, data_full, (((1,), (1,)), ((), ())), preferred_element_type=jnp.float32
    )
    sq_rows = jnp.einsum("rd,rd->r", piece, piece, preferred_element_type=jnp.float32)
    cross, sq_noise = (cross, sq_rows)
    cost = (sq_noise[:, None] + sq_data[None, :] - 2.0 * cross) / width
    g_pot = jnp.zeros((count_cols,), jnp.float32)
    for step in range(ITERS):
        f_pot = -EPS * row_lse((g_pot[None, :] - cost) / EPS)
        g_pot = -EPS * col_lse((f_pot[:, None] - cost) / EPS)
    scores = (g_pot[None, :] - cost) / EPS
    final = row_lse(scores)
    weights = jnp.exp(scores - final[:, None]).astype(jnp.bfloat16)
    targets = (
        lax.psum_scatter(
            lax.dot_general(
                data_full, weights, (((0,), (1,)), ((), ())), preferred_element_type=jnp.float32
            ).astype(jnp.bfloat16),
            "dp",
            scatter_dimension=0,
            tiled=True,
        )
        .astype(jnp.float32)
        .T
    )
    noise_f = noise.astype(jnp.float32)
    t_val = (timestep.astype(jnp.float32) + 0.5) / NBINS
    inputs_t = ((1.0 - t_val)[:, None] * noise_f + t_val[:, None] * targets).astype(jnp.bfloat16)
    velocity = (targets - noise_f).astype(jnp.bfloat16)
    return (inputs_t, velocity)


def solution(mesh):
    placed = (P("noise", "dp"), P("dp", "noise"), P("noise"))
    return jax.shard_map(
        per_device,
        mesh=mesh,
        in_specs=placed,
        out_specs=(P("noise", "dp"), P("noise", "dp")),
        check_vma=False,
    )
```

profile of v0, /device:TPU:6, one launch (start us, length us, event | category | flops | bytes accessed | tf_op | source)
XLA Modules:
  0.0 2313.5 jit_solution(10160644380432608850)
XLA Ops:
  7.2 0.7 all-gather.3.cloned.1.call-update
  7.9 0.7 all-gather.5.cloned.1.call-update
  8.7 229.9 %all-gather.3.cloned.1.call-done = bf16[64,16384]{1,0:T(8,128)(2,1)} async-done(((bf16[64,512]{1,0:T(8,128)(2,1)}), bf16[64,16384]{1,0:T(8,128)(2,1)}) %all-gather.3.cloned.1.call-update) | async-done | bytes 2097168 | tf_op jit(solution)/shard_map/all_gather | solution.py:32
  238.5 2.2 fusion.2
  240.8 177.6 %all-gather.5.cloned.1.call-done = bf16[256,16384]{1,0:T(8,128)(2,1)} async-done(((bf16[256,1024]{1,0:T(8,128)(2,1)}), bf16[256,16384]{1,0:T(8,128)(2,1)}) %all-gather.5.cloned.1.call-update) | async-done | bytes 8388624 | tf_op jit(solution)/shard_map/all_gather | solution.py:28
  418.4 5.3 fusion.1
  423.7 0.5 copy-done
  424.1 2.8 fusion.8
  426.9 114.2 %pmax.63 = f32[64]{0:T(128)S(1)} all-reduce(f32[64]{0:T(128)S(1)} %get-tuple-element.6), channel_id=1, replica_groups=mesh['noise'=16,'dp'=32] {'dp'}, use_global_device_ids=true, to_apply=%region_1.0 | all-reduce | flops 64 | bytes 512 | tf_op jit(solution)/shard_map/pmax | solution.py:15
  541.2 0.2 exponential_reduce_fusion.8
  541.4 113.4 %psum.63 = f32[64]{0:T(128)S(1)} all-reduce(f32[64]{0:T(128)S(1)} %exponential_reduce_fusion.8), channel_id=1, replica_groups=mesh['noise'=16,'dp'=32] {'dp'}, use_global_device_ids=true, to_apply=%region_3.0 | all-reduce | flops 64 | bytes 512 | tf_op jit(solution)/shard_map/psum | solution.py:16
  654.9 54.1 %pmax.64 = f32[256]{0:T(256)S(1)} all-reduce(f32[256]{0:T(256)S(1)} %fusion.9), channel_id=1, replica_groups=mesh['noise'=16,'dp'=32] {'noise'}, use_global_device_ids=true, to_apply=%region_5.0 | all-reduce | flops 256 | bytes 2048 | tf_op jit(solution)/shard_map/pmax | solution.py:22
  709.1 62.0 %psum.64 = f32[256]{0:T(256)S(1)} all-reduce(f32[256]{0:T(256)S(1)} %exponential_reduce_fusion.7), channel_id=1, replica_groups=mesh['noise'=16,'dp'=32] {'noise'}, use_global_device_ids=true, to_apply=%region_7.0 | all-reduce | flops 256 | bytes 2048 | tf_op jit(solution)/shard_map/psum | solution.py:23
  771.2 114.8 %pmax.65 = f32[64]{0:T(128)S(1)} all-reduce(f32[64]{0:T(128)S(1)} %fusion.10), channel_id=1, replica_groups=mesh['noise'=16,'dp'=32] {'dp'}, use_global_device_ids=true, to_apply=%region_9.0 | all-reduce | flops 64 | bytes 512 | tf_op jit(solution)/shard_map/pmax | solution.py:15
  886.2 112.8 %psum.65 = f32[64]{0:T(128)S(1)} all-reduce(f32[64]{0:T(128)S(1)} %exponential_reduce_fusion.6), channel_id=1, replica_groups=mesh['noise'=16,'dp'=32] {'dp'}, use_global_device_ids=true, to_apply=%region_11.0 | all-reduce | flops 64 | bytes 512 | tf_op jit(solution)/shard_map/psum | solution.py:16
  999.1 62.0 %pmax.66 = f32[256]{0:T(256)S(1)} all-reduce(f32[256]{0:T(256)S(1)} %fusion.11), channel_id=1, replica_groups=mesh['noise'=16,'dp'=32] {'noise'}, use_global_device_ids=true, to_apply=%region_13.0 | all-reduce | flops 256 | bytes 2048 | tf_op jit(solution)/shard_map/pmax | solution.py:22
  1061.2 62.0 %psum.66 = f32[256]{0:T(256)S(1)} all-reduce(f32[256]{0:T(256)S(1)} %exponential_reduce_fusion.5), channel_id=1, replica_groups=mesh['noise'=16,'dp'=32] {'noise'}, use_global_device_ids=true, to_apply=%region_15.0 | all-reduce | flops 256 | bytes 2048 | tf_op jit(solution)/shard_map/psum | solution.py:23
  1123.3 114.8 %pmax.67 = f32[64]{0:T(128)S(1)} all-reduce(f32[64]{0:T(128)S(1)} %fusion.12), channel_id=1, replica_groups=mesh['noise'=16,'dp'=32] {'dp'}, use_global_device_ids=true, to_apply=%region_17.0 | all-reduce | flops 64 | bytes 512 | tf_op jit(solution)/shard_map/pmax | solution.py:15
  1238.1 0.2 exponential_reduce_fusion.4
  1238.3 112.8 %psum.67 = f32[64]{0:T(128)S(1)} all-reduce(f32[64]{0:T(128)S(1)} %exponential_reduce_fusion.4), channel_id=1, replica_groups=mesh['noise'=16,'dp'=32] {'dp'}, use_global_device_ids=true, to_apply=%region_19.0 | all-reduce | flops 64 | bytes 512 | tf_op jit(solution)/shard_map/psum | solution.py:16
  1351.2 62.0 %pmax.68 = f32[256]{0:T(256)S(1)} all-reduce(f32[256]{0:T(256)S(1)} %fusion.13), channel_id=1, replica_groups=mesh['noise'=16,'dp'=32] {'noise'}, use_global_device_ids=true, to_apply=%region_21.0 | all-reduce | flops 256 | bytes 2048 | tf_op jit(solution)/shard_map/pmax | solution.py:22
  1413.3 62.0 %psum.68 = f32[256]{0:T(256)S(1)} all-reduce(f32[256]{0:T(256)S(1)} %exponential_reduce_fusion.3), channel_id=1, replica_groups=mesh['noise'=16,'dp'=32] {'noise'}, use_global_device_ids=true, to_apply=%region_23.0 | all-reduce | flops 256 | bytes 2048 | tf_op jit(solution)/shard_map/psum | solution.py:23
  1475.4 114.8 %pmax.69 = f32[64]{0:T(128)S(1)} all-reduce(f32[64]{0:T(128)S(1)} %fusion.14), channel_id=1, replica_groups=mesh['noise'=16,'dp'=32] {'dp'}, use_global_device_ids=true, to_apply=%region_25.0 | all-reduce | flops 64 | bytes 512 | tf_op jit(solution)/shard_map/pmax | solution.py:15
  1590.4 112.8 %psum.69 = f32[64]{0:T(128)S(1)} all-reduce(f32[64]{0:T(128)S(1)} %exponential_reduce_fusion.2), channel_id=1, replica_groups=mesh['noise'=16,'dp'=32] {'dp'}, use_global_device_ids=true, to_apply=%region_27.0 | all-reduce | flops 64 | bytes 512 | tf_op jit(solution)/shard_map/psum | solution.py:16
  1703.3 62.0 %pmax.70 = f32[256]{0:T(256)S(1)} all-reduce(f32[256]{0:T(256)S(1)} %fusion.15), channel_id=1, replica_groups=mesh['noise'=16,'dp'=32] {'noise'}, use_global_device_ids=true, to_apply=%region_29.0 | all-reduce | flops 256 | bytes 2048 | tf_op jit(solution)/shard_map/pmax | solution.py:22
  1765.4 62.0 %psum.70 = f32[256]{0:T(256)S(1)} all-reduce(f32[256]{0:T(256)S(1)} %exponential_reduce_fusion.1), channel_id=1, replica_groups=mesh['noise'=16,'dp'=32] {'noise'}, use_global_device_ids=true, to_apply=%region_31.0 | all-reduce | flops 256 | bytes 2048 | tf_op jit(solution)/shard_map/psum | solution.py:23
  1827.5 114.8 %pmax.71 = f32[64]{0:T(128)S(1)} all-reduce(f32[64]{0:T(128)S(1)} %fusion.16), channel_id=1, replica_groups=mesh['noise'=16,'dp'=32] {'dp'}, use_global_device_ids=true, to_apply=%region_33.0 | all-reduce | flops 64 | bytes 512 | tf_op jit(solution)/shard_map/pmax | solution.py:15
  1942.3 0.2 exponential_reduce_fusion
  1942.5 112.8 %psum.71 = f32[64]{0:T(128)S(1)} all-reduce(f32[64]{0:T(128)S(1)} %exponential_reduce_fusion), channel_id=1, replica_groups=mesh['noise'=16,'dp'=32] {'dp'}, use_global_device_ids=true, to_apply=%region_35.0 | all-reduce | flops 64 | bytes 512 | tf_op jit(solution)/shard_map/psum | solution.py:16
  2055.3 6.4 fusion
  2061.8 243.7 %reduce-scatter.2.cloned.1.call-done = bf16[512,64]{0,1:T(8,128)(2,1)} async-done(((bf16[16384,64]{0,1:T(8,128)(2,1)}), bf16[512,64]{0,1:T(8,128)(2,1)}) %reduce-scatter.2.cloned.1.call-update) | async-done | bytes 65552 | tf_op jit(solution)/shard_map/reduce_scatter | solution.py:47
  2305.4 1.6 fusion.7
  (35 shorter events, 1.9 us)
Async XLA Ops:
  7.2 231.4 %all-gather.3.cloned.1.call-start = ((), (), s32[]{:S(2)}) async-start(), calls=%async_computation.1 | async-start | bytes 2162688 | tf_op jit(solution)/shard_map/all_gather | solution.py:32
  7.9 410.5 %all-gather.5.cloned.1.call-start = ((), (), s32[]{:S(2)}) async-start(), calls=%async_computation.2 | async-start | bytes 8912896 | tf_op jit(solution)/shard_map/all_gather | solution.py:28
  8.6 2296.8 %reduce-scatter.2.cloned.1.call-start = ((), (), s32[]{:S(2)}) async-start(), calls=%async_computation.3 | async-start | bytes 2162688 | tf_op jit(solution)/shard_map/reduce_scatter | solution.py:47
  238.5 185.1 %copy-start.1 = (bf16[64,16384]{1,0:T(8,128)(2,1)S(1)}, bf16[64,16384]{1,0:T(8,128)(2,1)}, u32[]{:S(2)}) copy-start(bf16[64,16384]{1,0:T(8,128)(2,1)} %all-gather.3.cloned.1.call-done) | copy-start | bytes 6291460
  418.4 5.8 copy-start
  426.9 1634.8 %copy-start.3 = (s32[64]{0:T(128)S(1)}, s32[64]{0:T(128)}, u32[]{:S(2)}) copy-start(s32[64]{0:T(128)} %param.5) | copy-start | bytes 772
  426.9 1878.5 %copy-start.2 = (bf16[64,512]{1,0:T(8,128)(2,1)S(1)}, bf16[64,512]{1,0:T(8,128)(2,1)}, u32[]{:S(2)}) copy-start(bf16[64,512]{1,0:T(8,128)(2,1)} %param.3) | copy-start | bytes 196612
Sparse Core Ops, SparseCore 0:
  10.1 228.4 all-gather.2
  241.9 176.4 all-gather.4
  2061.9 243.5 reduce-scatter.1
where the time goes:
time: 2310 us
  blocking collectives  1630 us (71%)
  waiting for transfers between devices  652 us (28%)
    pmax x5, blocking collectives, row_lse(): peak = lax.pmax(local_peak, 'dp')  573 us
    psum x5, blocking collectives, row_lse(): total = lax.psum(jnp.sum(jnp.exp(scores - peak[:, None]), axis=1), 'dp')  565 us
    psum x4, blocking collectives, col_lse(): total = lax.psum(jnp.sum(jnp.exp(scores - peak[None, :]), axis=0), 'noise')  248 us
    reduce_scatter x1, waiting for transfers between devices, per_device(): lax.psum_scatter(lax.dot_general(data_full, weights, (((0,), (1,)), ((),...  244 us
    pmax x4, blocking collectives, col_lse(): peak = lax.pmax(local_peak, 'noise')  240 us
    all_gather x1, waiting for transfers between devices, per_device(): piece = lax.all_gather(noise, 'dp', axis=1, tiled=True)  230 us
    all_gather x1, waiting for transfers between devices, per_device(): data_full = lax.all_gather(data, 'noise', axis=1, tiled=True)  178 us
  transfers between devices with their start and end apart: 3, of which 3 were waited for; matrix products, arithmetic and copies ran while one was open for 0% of the time, Pallas kernels for 0%

commit v1 on v0

v1 whole, which is shorter than its diff:
```python
import functools

import jax
import jax.numpy as jnp
from jax import lax
from jax.experimental import pallas as pl
from jax.experimental.pallas import tpu as pltpu
from jax.sharding import PartitionSpec as P

ITERS = 4
NBINS = 1000
EPS = 0.002
LOG2E = 1.4426950408889634
MESH = pl.DeviceIdType.MESH
VMEM = pltpu.VMEM
F32 = jnp.float32
BF16 = jnp.bfloat16


def place():
    n, d = lax.axis_index("noise"), lax.axis_index("dp")
    return n, d, n // 8, (n // 2) % 4, n % 2, d // 4, d % 4


def greet(peers):
    barrier = pltpu.get_barrier_semaphore()
    for peer in peers:
        pl.semaphore_signal(barrier, inc=1, device_id=peer, device_id_type=MESH)
    return barrier


def remote(src, dst, send, recv, peer):
    return pltpu.make_async_remote_copy(
        src_ref=src, dst_ref=dst, send_sem=send, recv_sem=recv, device_id=peer, device_id_type=MESH
    )


def b2i(cond):
    return jnp.where(cond, 1, 0).astype(jnp.int32)


def cost_kernel(scale, noise_ref, data_ref, s_ref, buf, part, half, xin, zin, own, tot,
                first_send, arrive, send, c_send, c_recv, x_send, x_recv, z_send, z_recv,
                gx_send, gx_recv, gc_send, gc_recv):
    n, d, zh, x, c, zl, y = place()
    other = (n + 1 - 2 * c, d)
    far = (lax.rem(n + 8, 16), d)

    def xpeer(k):
        return zh * 8 + lax.rem(x + k, 4) * 2 + c

    up = (n, lax.rem(zl + 1, 8) * 4 + y)
    down = (n, lax.rem(zl + 7, 8) * 4 + y)
    yup = (n, zl * 4 + lax.rem(y + 1, 4))
    ydown = (n, zl * 4 + lax.rem(y + 3, 4))
    head_n, head_d, head_h = d // 2, 28 * c + y, y % 2
    mine = jnp.logical_and(head_n == n, head_d == d)
    is_head = jnp.logical_and(c == y // 2, jnp.logical_or(zl == 0, zl == 7))

    barrier = greet([other, far, up, down, yup, ydown] + [(xpeer(k), d) for k in (1, 2, 3)])

    src_d = (4 * zh + x) * 4 + y
    src_c = zl // 7

    @pl.when(is_head)
    def _():
        for k in range(8):
            src_n = k * 2 + src_c

            @pl.when(jnp.logical_not(jnp.logical_and(src_n == n, src_d == d)))
            def _():
                pl.semaphore_signal(barrier, inc=1, device_id=(src_n, src_d), device_id_type=MESH)

    pl.semaphore_wait(barrier, 9 + b2i(jnp.logical_not(mine)))

    def first():
        return remote(noise_ref, buf.at[head_h, n], first_send, arrive.at[head_h, n], (head_n, head_d))

    @pl.when(jnp.logical_not(mine))
    def _():
        first().start()

    @pl.when(mine)
    def _():
        pltpu.make_async_copy(noise_ref, buf.at[head_h, n], arrive.at[head_h, n]).start()

    def landed(h, b):
        pltpu.make_async_copy(noise_ref, buf.at[h, b], arrive.at[h, b]).wait()

    def hop(h, b, kind, peer):
        return remote(buf.at[h, b], buf.at[h, b], send.at[h, b, kind], arrive.at[h, b], peer)

    def forwards(h, b, j, direction, act):
        r = lax.rem(y - (2 * c + h) + 4, 4)
        on_chain = r == 0
        if direction == 0:
            more, nxt = zl < 7, up
        else:
            more, nxt = zl > 0, down

        @pl.when(jnp.logical_and(on_chain, more))
        def _():
            act(hop(h, b, 0, nxt))

        @pl.when(jnp.logical_or(on_chain, jnp.logical_and(r == 1, j < 4)))
        def _():
            act(hop(h, b, 1, yup))

        @pl.when(jnp.logical_or(on_chain, jnp.logical_and(r == 3, j >= 4)))
        def _():
            act(hop(h, b, 2, ydown))

    def tick(t, carry):
        for direction in (0, 1):
            pos = zl if direction == 0 else 7 - zl
            for h in (0, 1):
                r = lax.rem(y - (2 * c + h) + 4, 4)
                j = t - pos - b2i(r != 0)

                @pl.when(jnp.logical_and(r != 2, jnp.logical_and(j >= 0, j < 8)))
                def _():
                    b = 2 * j + direction
                    landed(h, b)
                    forwards(h, b, j, direction, lambda cp: cp.start())
        return carry

    lax.fori_loop(0, 16, tick, 0)

    def rest(j, carry):
        for direction in (0, 1):
            for h in (0, 1):
                r = lax.rem(y - (2 * c + h) + 4, 4)
                b = 2 * j + direction

                @pl.when(r == 2)
                def _():
                    landed(h, b)

                forwards(h, b, j, direction, lambda cp: cp.wait_send())
        return carry

    lax.fori_loop(0, 8, rest, 0)

    @pl.when(jnp.logical_not(mine))
    def _():
        first().wait_send()

    data = data_ref[...]
    dsq = jnp.sum(jnp.square(data.astype(F32)), axis=1, keepdims=True)
    ones = jnp.ones((8, 512), BF16)

    def block(b, carry):
        acc = jnp.broadcast_to(dsq, (256, 128))
        nsq = jnp.zeros((8, 128), F32)
        for h in (0, 1):
            piece = buf[h, pl.ds(2 * b, 2)].reshape(128, 512)
            acc -= 2.0 * lax.dot_general(
                data_ref[:, 512 * h:512 * (h + 1)], piece, (((1,), (1,)), ((), ())), preferred_element_type=F32
            )
            wide = piece.astype(F32)
            sq = wide * wide
            hi = sq.astype(BF16)
            lo = (sq - hi.astype(F32)).astype(BF16)
            for v in (hi, lo):
                nsq += lax.dot_general(ones, v, (((1,), (1,)), ((), ())), preferred_element_type=F32)
        part[b] = (acc + nsq[0:1, :]) * scale
        return carry

    lax.fori_loop(0, 8, block, 0)

    cp = remote(part.at[pl.ds(4 * (1 - c), 4)], half, c_send, c_recv, other)
    cp.start()
    cp.wait()
    for k in range(4):
        half[k] = half[k] + part[4 * c + k]
    for k in (1, 2, 3):
        t = lax.rem(x + k, 4)
        remote(half.at[t], xin.at[x], x_send.at[k], x_recv.at[x], (xpeer(k), d)).start()
    acc = half[x]
    for k in (1, 2, 3):
        t = lax.rem(x + k, 4)
        remote(half.at[t], xin.at[t], x_send.at[k], x_recv.at[t], (xpeer(k), d)).wait()
        acc += xin[t]
    own[...] = acc
    cp = remote(own, zin, z_send, z_recv, far)
    cp.start()
    cp.wait()
    tot[4 * c + x] = own[...] + zin[...]
    mineb = tot.at[4 * c + x]
    for k in (1, 2, 3):
        remote(mineb, mineb, gx_send.at[k], gx_recv.at[x], (xpeer(k), d)).start()
    for k in (1, 2, 3):
        t = lax.rem(x + k, 4)
        remote(mineb, tot.at[4 * c + t], gx_send.at[k], gx_recv.at[t], (xpeer(k), d)).wait()
    cp = remote(tot.at[pl.ds(4 * c, 4)], tot.at[pl.ds(4 * c, 4)], gc_send, gc_recv, other)
    cp.start()
    cp.wait_send()
    remote(tot.at[pl.ds(4 * (1 - c), 4)], tot.at[pl.ds(4 * (1 - c), 4)], gc_send, gc_recv, other).wait_recv()
    s_ref[...] = tot[...]


def sinkhorn_kernel(s_ref, data_ref, w_ref, dt_ref, gpot, row, rz, ry, zs, zr, ys, yr, as_, ar, loc):
    n, d, zh, x, c, zl, y = place()

    def zp(k):
        return lax.rem(zl + k, 8)

    def yp(k):
        return lax.rem(y + k, 4)

    zpeers = [(n, zp(k) * 4 + y) for k in range(1, 8)]
    ypeers = [(n, zl * 4 + yp(k)) for k in range(1, 4)]
    dests = []
    for h in (0, 1):
        for cc in (0, 1):
            dests.append((h, cc, (zh * 8 + x * 2 + cc, zl * 4 + 2 * c + h)))
    srcc = y // 2
    srcs = [(zh * 8 + x * 2 + srcc, zl * 4 + k) for k in range(4)]
    barrier = greet(zpeers + ypeers)
    for k in range(4):
        same = jnp.logical_and(srcc == c, y == k)

        @pl.when(jnp.logical_not(same))
        def _():
            pl.semaphore_signal(barrier, inc=1, device_id=srcs[k], device_id_type=MESH)

    count = 10
    for h, cc, _ in dests:
        count = count + 1 - b2i(jnp.logical_and(c == cc, y == 2 * c + h))
    pl.semaphore_wait(barrier, count)

    def spread(h, cc, peer, act):
        same = jnp.logical_and(c == cc, y == 2 * c + h)
        src = data_ref.at[:, pl.ds(512 * h, 512)]

        @pl.when(jnp.logical_not(same))
        def _():
            act(remote(src, dt_ref.at[y], as_.at[h, cc], ar.at[y], peer))

        @pl.when(same)
        def _():
            act(pltpu.make_async_copy(src, dt_ref.at[y], loc), True)

    for h, cc, peer in dests:
        spread(h, cc, peer, lambda cp, own=False: cp.start())

    gpot[...] = jnp.zeros_like(gpot)

    def rows(k):
        g = gpot[...]
        for b in range(8):
            v = g - s_ref[b]
            m = jnp.max(v, axis=0, keepdims=True)
            row[k, b:b + 1, :] = m + jnp.log2(jnp.sum(jnp.exp2(v - m), axis=0, keepdims=True))
        for i, peer in enumerate(zpeers):
            remote(row.at[k], rz.at[k, zl], zs.at[k, i], zr.at[k, zl], peer).start()
        rz[k, zl] = row[k]
        for i, peer in enumerate(zpeers):
            remote(row.at[k], rz.at[k, zp(i + 1)], zs.at[k, i], zr.at[k, zp(i + 1)], peer).wait()
        v = rz[k]
        m = jnp.max(v, axis=0)
        ry[k, y] = m + jnp.log2(jnp.sum(jnp.exp2(v - m[None]), axis=0))
        mine = ry.at[k, y]
        for i, peer in enumerate(ypeers):
            remote(mine, mine, ys.at[k, i], yr.at[k, y], peer).start()
        for i, peer in enumerate(ypeers):
            remote(mine, ry.at[k, yp(i + 1)], ys.at[k, i], yr.at[k, yp(i + 1)], peer).wait()
        v = ry[k]
        m = jnp.max(v, axis=0)
        return m + jnp.log2(jnp.sum(jnp.exp2(v - m[None]), axis=0))

    def iteration(k, carry):
        lse = rows(k)
        m = (-lse[0:1]) - s_ref[0]
        for b in range(1, 8):
            m = jnp.maximum(m, (-lse[b:b + 1]) - s_ref[b])
        m = jnp.broadcast_to(jnp.max(m, axis=1, keepdims=True), (256, 128))
        tot = jnp.zeros((256, 128), F32)
        for b in range(8):
            tot += jnp.exp2((-lse[b:b + 1]) - s_ref[b] - m)
        tot = jnp.broadcast_to(jnp.sum(tot, axis=1, keepdims=True), (256, 128))
        gpot[...] = -(m + jnp.log2(tot))
        return carry

    lax.fori_loop(0, ITERS, iteration, 0)
    lse = rows(ITERS)
    g = gpot[...]
    for b in range(8):
        w_ref[b] = jnp.exp2(g - s_ref[b] - lse[b:b + 1]).astype(BF16)

    for h, cc, peer in dests:
        spread(h, cc, peer, lambda cp, own=False: cp.wait() if own else cp.wait_send())
    for k in range(4):
        same = jnp.logical_and(srcc == c, y == k)

        @pl.when(jnp.logical_not(same))
        def _():
            remote(dt_ref.at[k], dt_ref.at[k], as_.at[0, 0], ar.at[k], srcs[k]).wait_recv()


def target_kernel(w_ref, dt_ref, t_ref, wbuf, part, inbox, stage, got, ws, wr, cs, cr, fs, fr):
    n, d, zh, x, c, zl, y = place()
    up = (n, lax.rem(zl + 1, 8) * 4 + y)
    down = (n, lax.rem(zl + 7, 8) * 4 + y)
    yup = (n, zl * 4 + lax.rem(y + 1, 4))
    ydown = (n, zl * 4 + lax.rem(y + 3, 4))
    out_d = 16 * zh + 4 * x + y
    from_n = (zl // 4) * 8 + (zl % 4) * 2 + zh
    from_d = 28 * (1 - c) + y
    from_self = jnp.logical_and(from_n == n, from_d == d)
    barrier = greet([up, down, yup, ydown])

    @pl.when(jnp.logical_not(from_self))
    def _():
        pl.semaphore_signal(barrier, inc=1, device_id=(from_n, from_d), device_id_type=MESH)

    is_end = jnp.logical_or(zl == 0, zl == 7)
    self_end = b2i(jnp.logical_and(is_end, from_self))
    pl.semaphore_wait(barrier, 4 + 4 * b2i(is_end) - self_end)

    rows4 = pl.ds(4 * c, 4)
    mine = w_ref.at[rows4]

    def wsend(q, dst_y, k, peer):
        src = mine if dst_y is None else wbuf.at[dst_y]
        slot = wbuf.at[y] if dst_y is None else wbuf.at[dst_y]
        lo = pl.ds(2 * q, 2)
        return remote(src.at[lo], slot.at[lo], ws.at[k, q], wr.at[y if dst_y is None else dst_y, q], peer)

    left, right, across = lax.rem(y + 3, 4), lax.rem(y + 1, 4), lax.rem(y + 2, 4)
    for q in (0, 1):
        wsend(q, None, 0, yup).start()
    for q in (1, 0):
        wsend(q, None, 1, ydown).start()
    wbuf[y] = w_ref[rows4]

    def wwait(src_y, q):
        lo = pl.ds(2 * q, 2)
        remote(mine.at[lo], wbuf.at[src_y].at[lo], ws.at[0, q], wr.at[src_y, q], yup).wait_recv()

    wwait(left, 0)
    wsend(0, left, 2, yup).start()
    wwait(right, 1)
    wsend(1, right, 3, ydown).start()
    wwait(left, 1)
    wwait(right, 0)
    wwait(across, 0)
    wwait(across, 1)

    def mul(b, carry):
        acc = jnp.zeros((128, 512), F32)
        for k in range(4):
            acc += lax.dot_general(
                wbuf[k, b], dt_ref[k], (((0,), (0,)), ((), ())), preferred_element_type=F32
            )
        part[pl.ds(2 * b, 2)] = acc.reshape(2, 64, 512)
        return carry

    lax.fori_loop(0, 4, mul, 0)

    def hop(b, direction):
        return remote(stage.at[b], inbox.at[b], cs.at[b], cr.at[b], up if direction == 0 else down)

    def final(b):
        return remote(stage.at[b], got, fs.at[b], fr, (8 * c + b, out_d))

    def own_end(b):
        return jnp.logical_and(n == 8 * c + b, d == out_d)

    def tick(t, carry):
        for direction in (0, 1):
            pos = zl if direction == 0 else 7 - zl
            j = t - pos
            b = 2 * j + direction

            @pl.when(jnp.logical_and(j >= 0, j < 4))
            def _():
                @pl.when(pos == 0)
                def _():
                    stage[b] = part[b].astype(BF16)

                @pl.when(pos > 0)
                def _():
                    hop(b, direction).wait_recv()
                    stage[b] = (part[b] + inbox[b].astype(F32)).astype(BF16)

                @pl.when(pos < 7)
                def _():
                    hop(b, direction).start()

                @pl.when(pos == 7)
                def _():
                    @pl.when(jnp.logical_not(own_end(b)))
                    def _():
                        final(b).start()

                    @pl.when(own_end(b))
                    def _():
                        pltpu.make_async_copy(stage.at[b], got, fr).start()
        return carry

    lax.fori_loop(0, 11, tick, 0)
    pltpu.make_async_copy(stage.at[0], got, fr).wait()
    t_ref[...] = got[...]

    def drain(j, carry):
        for direction in (0, 1):
            pos = zl if direction == 0 else 7 - zl
            b = 2 * j + direction

            @pl.when(pos < 7)
            def _():
                hop(b, direction).wait_send()

            @pl.when(jnp.logical_and(pos == 7, jnp.logical_not(own_end(b))))
            def _():
                final(b).wait_send()
        return carry

    lax.fori_loop(0, 4, drain, 0)
    for q in (0, 1):
        wsend(q, None, 0, yup).wait_send()
        wsend(q, None, 1, ydown).wait_send()
    wsend(0, left, 2, yup).wait_send()
    wsend(1, right, 3, ydown).wait_send()


def whole():
    return pl.BlockSpec(memory_space=pltpu.VMEM)


def params(cid):
    return pltpu.CompilerParams(collective_id=cid, has_side_effects=True, vmem_limit_bytes=40 * 1024 * 1024)


DMA = pltpu.SemaphoreType.DMA


def cost_call(noise, data):
    scale = LOG2E / (16384.0 * EPS)
    return pl.pallas_call(
        functools.partial(cost_kernel, scale),
        out_shape=jax.ShapeDtypeStruct((8, 256, 128), F32),
        in_specs=[whole()] * 2,
        out_specs=whole(),
        scratch_shapes=[
            VMEM((2, 16, 64, 512), BF16),
            VMEM((8, 256, 128), F32),
            VMEM((4, 256, 128), F32),
            VMEM((4, 256, 128), F32),
            VMEM((256, 128), F32),
            VMEM((256, 128), F32),
            VMEM((8, 256, 128), F32),
            DMA, DMA((2, 16)), DMA((2, 16, 3)),
            DMA, DMA, DMA((4,)), DMA((4,)), DMA, DMA,
            DMA((4,)), DMA((4,)), DMA, DMA,
        ],
        compiler_params=params(1),
    )(noise, data)


def sinkhorn_call(s, data):
    return pl.pallas_call(
        sinkhorn_kernel,
        out_shape=[jax.ShapeDtypeStruct((8, 256, 128), BF16), jax.ShapeDtypeStruct((4, 256, 512), BF16)],
        in_specs=[whole()] * 2,
        out_specs=[whole()] * 2,
        scratch_shapes=[
            VMEM((256, 128), F32),
            VMEM((ITERS + 1, 8, 128), F32),
            VMEM((ITERS + 1, 8, 8, 128), F32),
            VMEM((ITERS + 1, 4, 8, 128), F32),
            DMA((ITERS + 1, 7)), DMA((ITERS + 1, 8)),
            DMA((ITERS + 1, 3)), DMA((ITERS + 1, 4)),
            DMA((2, 2)), DMA((4,)), DMA,
        ],
        compiler_params=params(2),
    )(s, data)


def target_call(w, dt):
    return pl.pallas_call(
        target_kernel,
        out_shape=jax.ShapeDtypeStruct((64, 512), BF16),
        in_specs=[whole()] * 2,
        out_specs=whole(),
        scratch_shapes=[
            VMEM((4, 4, 256, 128), BF16),
            VMEM((8, 64, 512), F32),
            VMEM((8, 64, 512), BF16),
            VMEM((8, 64, 512), BF16),
            VMEM((64, 512), BF16),
            DMA((4, 2)), DMA((4, 2)),
            DMA((8,)), DMA((8,)), DMA((8,)), DMA,
        ],
        compiler_params=params(3),
    )(w, dt)


def per_device(noise, data, timestep):
    s = cost_call(noise, data)
    w, dt = sinkhorn_call(s, data)
    targets = target_call(w, dt).astype(F32)
    noise_f = noise.astype(F32)
    t_val = (timestep.astype(F32) + 0.5) / NBINS
    inputs_t = ((1.0 - t_val)[:, None] * noise_f + t_val[:, None] * targets).astype(BF16)
    velocity = (targets - noise_f).astype(BF16)
    return (inputs_t, velocity)


def solution(mesh):
    placed = (P("noise", "dp"), P("dp", "noise"), P("noise"))
    return jax.shard_map(
        per_device,
        mesh=mesh,
        in_specs=placed,
        out_specs=(P("noise", "dp"), P("noise", "dp")),
        check_vma=False,
    )
```

time: 2310 us -> 234 us (0.10)
  blocking collectives: 1630 us -> 0 us
  waiting for transfers between devices: 652 us -> 0 us
  Pallas kernels: 0 us -> 230 us
    pmax x9 -> x0, blocking collectives: 813 us -> none  [the longest x5 573 us: row_lse(): peak = lax.pmax(local_peak, 'dp')]
    psum x9 -> x0, blocking collectives: 813 us -> none  [the longest x5 565 us: row_lse(): total = lax.psum(jnp.sum(jnp.exp(scores - peak[:, None]), axis=1), 'dp')]
    all_gather x2 -> x0, waiting for transfers between devices: 407 us -> none  [the longest x1 230 us: per_device(): piece = lax.all_gather(noise, 'dp', axis=1, tiled=True)]
    reduce_scatter x1 -> x0, waiting for transfers between devices: 244 us -> none  [per_device(): lax.psum_scatter(lax.dot_general(data_full, weights, (((0,), (1,)), ((),...]
    pallas_call x0 -> x3, Pallas kernels: none -> 230 us  [the longest x1 110 us: cost_call(): pl.pallas_call(functools.partial(cost_kernel, scale), out_shape=jax.Shape...]
  transfers between devices with their start and end apart: 3 -> 0, of which waited for: 3 -> 0; matrix products, arithmetic and copies ran while one was open for 0% -> 0% of each run, Pallas kernels for 0% -> 0%
where the time goes in v1:
time: 234 us; the launch traced here: 233 us
  Pallas kernels  230 us (98%)
    pallas_call x1, Pallas kernels, cost_call(): pl.pallas_call(functools.partial(cost_kernel, scale), out_shape=jax.Shape...  110 us
    pallas_call x1, Pallas kernels, sinkhorn_call(): pl.pallas_call(sinkhorn_kernel, out_shape=[jax.ShapeDtypeStruct((8, 256,...  61.1 us
    pallas_call x1, Pallas kernels, target_call(): pl.pallas_call(target_kernel, out_shape=jax.ShapeDtypeStruct((64, 512), B...  59 us

profile of v1, /device:TPU:6, one launch (start us, length us, event | category | flops | bytes accessed | tf_op | source)
XLA Modules:
  0.0 233.4 jit_solution(16390846364260185229)
XLA Ops:
  0.6 0.0 copy-start
  0.6 1.0 copy-done
  1.7 0.0 copy-start.1
  1.7 0.8 copy-done.1
  2.5 110.0 %shard_map.50.s_ref = f32[8,256,128]{2,1,0:T(8,128)S(1)} custom-call(bf16[64,512]{1,0:T(8,128)(2,1)S(1)} %copy-done.1, bf16[256,1024]{1,0:T(8,128)(2,1)S(1)} %copy-done), custom_call_target="tpu_custom_call" | custom-call | tf_op jit(solution)/shard_map/pallas_call | solution.py:441
  112.5 61.1 %shard_map.51 = (bf16[8,256,128]{2,1,0:T(8,128)(2,1)S(1)}, bf16[4,256,512]{2,1,0:T(8,128)(2,1)S(1)}) custom-call(f32[8,256,128]{2,1,0:T(8,128)S(1)} %shard_map.50.s_ref, bf16[256,1024]{1,0:T(8,128)(2,1)S(1)} %copy-done), custom_call_target="tpu_custom_call" | custom-call | tf_op jit(solution)/shard_map/pallas_call | solution.py:463
  173.6 0.0 copy-start.2
  173.6 59.0 %shard_map.52 = bf16[64,512]{1,0:T(8,128)(2,1)S(1)} custom-call(bf16[8,256,128]{2,1,0:T(8,128)(2,1)S(1)} %get-tuple-element.4.w_ref, bf16[4,256,512]{2,1,0:T(8,128)(2,1)S(1)} %get-tuple-element.5.dt_ref), custom_call_target="tpu_custom_call" | custom-call | tf_op jit(solution)/shard_map/pallas_call | solution.py:482
  232.7 0.0 copy-done.2
  232.7 0.7 fusion.2
  (1 shorter events, 0.0 us)
Async XLA Ops:
  0.6 1.0 copy-start
  1.7 0.8 copy-start.1
  173.6 59.1 %copy-start.2 = (s32[64]{0:T(128)S(1)}, s32[64]{0:T(128)}, u32[]{:S(2)}) copy-start(s32[64]{0:T(128)} %param.5) | copy-start | bytes 772

commit v2 on v0

v2 whole, which is shorter than its diff:
```python
import functools

import jax
import jax.numpy as jnp
from jax import lax
from jax.experimental import pallas as pl
from jax.experimental.pallas import tpu as pltpu
from jax.sharding import PartitionSpec as P

ITERS = 4
NBINS = 1000
EPS = 0.002
LOG2E = 1.4426950408889634
MESH = pl.DeviceIdType.MESH
VMEM = pltpu.VMEM
F32 = jnp.float32
BF16 = jnp.bfloat16
LAG = 4


def remote(src, dst, send, recv, peer):
    return pltpu.make_async_remote_copy(
        src_ref=src, dst_ref=dst, send_sem=send, recv_sem=recv, device_id=peer, device_id_type=MESH
    )


def b2i(cond):
    return jnp.where(cond, 1, 0).astype(jnp.int32)


def fused_kernel(scale, noise_hbm, data_hbm, out_ref,
                 noise_ref, data_ref, dsq_ref, buf, part, half, xin, own, zin, s_ref,
                 gpot, row, rz, ry, mloc, w_ref, dt_ref, wbuf, mbuf, tpart, stage, qin, fin, got,
                 load_sem, first_send, arrive, send,
                 c_send, c_recv, x_send, x_recv, z_send, z_recv, gx_send, gx_recv, gc_send, gc_recv,
                 zs, zr, ys, yr, as_, ar, loc, ws, wr, ms, mr, qs, qr, fs, fr):
    n, d = lax.axis_index("noise"), lax.axis_index("dp")
    zh, x, c, zl, y = n // 8, (n // 2) % 4, n % 2, d // 4, d % 4
    load_noise = pltpu.make_async_copy(noise_hbm, noise_ref, load_sem.at[0])
    load_data = pltpu.make_async_copy(data_hbm, data_ref, load_sem.at[1])
    load_noise.start()
    load_data.start()

    other_n = n + 1 - 2 * c
    other = (other_n, d)
    far = (lax.rem(n + 8, 16), d)

    def xq(k):
        return lax.rem(x + k, 4)

    def yq(k):
        return lax.rem(y + k, 4)

    def zq(k):
        return lax.rem(zl + k, 8)

    xpeers = [(zh * 8 + xq(k) * 2 + c, d) for k in (1, 2, 3)]
    ypeers = [(n, zl * 4 + yq(k)) for k in (1, 2, 3)]
    zpeers = [(n, zq(k) * 4 + y) for k in range(1, 8)]
    yup, ydown = ypeers[0], ypeers[2]
    across = [(other_n, zl * 4 + yq(k)) for k in (1, 2, 3)]
    zup, zdown = zpeers[0], zpeers[6]
    zi, zg = zl % 4, zl // 4

    head_n, head_h = d // 2, y % 2
    heads = [(head_n, (4 * g + 3 * c) * 4 + y) for g in (0, 1)]
    q_me = c * 8 + zh * 4 + x

    def is_me(peer):
        return jnp.logical_and(peer[0] == n, peer[1] == d)

    barrier = pltpu.get_barrier_semaphore()

    def greet(peer):
        pl.semaphore_signal(barrier, inc=1, device_id=peer, device_id_type=MESH)

    sym = [other, far] + xpeers + ypeers + zpeers + across
    for peer in sym:
        greet(peer)
    is_head = jnp.logical_and(c == y // 2, jnp.logical_or(zi == 0, zi == 3))

    @pl.when(is_head)
    def _():
        for k in range(8):
            peer = (k * 2 + zi // 3, (4 * zh + x) * 4 + y)

            @pl.when(jnp.logical_not(is_me(peer)))
            def _():
                greet(peer)

    final_from = [((zl // 4) * 8 + zi * 2 + c, (x + 4 * g) * 4 + y) for g in (0, 1)]
    final_to = [(h * 8 + zi * 2 + c, (4 * zh + x) * 4 + y) for h in (0, 1)]
    count = len(sym)
    for peer in final_from:
        @pl.when(jnp.logical_not(is_me(peer)))
        def _():
            greet(peer)
    for peer in heads + final_to:
        count = count + 1 - b2i(is_me(peer))
    load_noise.wait()
    pl.semaphore_wait(barrier, count)

    def first(g):
        return remote(noise_ref, buf.at[head_h, q_me], first_send.at[g], arrive.at[head_h, q_me], heads[g])

    for g in (0, 1):
        @pl.when(jnp.logical_not(is_me(heads[g])))
        def _():
            first(g).start()

        @pl.when(is_me(heads[g]))
        def _():
            pltpu.make_async_copy(noise_ref, buf.at[head_h, q_me], arrive.at[head_h, q_me]).start()

    load_data.wait()
    dsq_ref[...] = jnp.broadcast_to(
        jnp.sum(jnp.square(data_ref[...].astype(F32)), axis=1, keepdims=True), (256, 128)
    )

    def landed(h, q):
        pltpu.make_async_copy(noise_ref, buf.at[h, q], arrive.at[h, q]).wait()

    def hop(h, q, kind, peer):
        return remote(buf.at[h, q], buf.at[h, q], send.at[h, q, kind], arrive.at[h, q], peer)

    def around(h):
        return lax.rem(y - (2 * c + h) + 4, 4)

    def forwards(h, q, act):
        r = around(h)
        j, upward = q % 8, q < 8
        on_chain = r == 0

        @pl.when(jnp.logical_and(on_chain, jnp.logical_and(upward, zi < 3)))
        def _():
            act(hop(h, q, 0, zup))

        @pl.when(jnp.logical_and(on_chain, jnp.logical_and(jnp.logical_not(upward), zi > 0)))
        def _():
            act(hop(h, q, 0, zdown))

        @pl.when(jnp.logical_or(on_chain, jnp.logical_and(r == 1, j % 2 == 0)))
        def _():
            act(hop(h, q, 1, yup))

        @pl.when(jnp.logical_or(on_chain, jnp.logical_and(r == 3, j % 2 == 1)))
        def _():
            act(hop(h, q, 2, ydown))

    near = zi // 2

    def side(k):
        return near if k == 0 else 1 - near

    def tick(t, carry):
        for lagging in (0, 1):
            for h in (0, 1):
                r = around(h)
                s = t - LAG * lagging
                mine = r == 0 if lagging == 0 else jnp.logical_or(r == 1, r == 3)

                @pl.when(jnp.logical_and(mine, jnp.logical_and(s >= 0, s < 16)))
                def _():
                    q = 8 * jnp.where(s < 8, near, 1 - near) + s % 8
                    landed(h, q)
                    forwards(h, q, lambda cp: cp.start())
        return carry

    def last_column(k):
        def body(j, carry):
            for h in (0, 1):
                @pl.when(around(h) == 2)
                def _():
                    landed(h, 8 * side(k) + j)
            return carry

        lax.fori_loop(0, 8, body, 0)

    ones = jnp.ones((8, 512), BF16)

    def costs(k):
        def block(b, carry):
            acc = dsq_ref[...]
            nsq = jnp.zeros((8, 128), F32)
            for h in (0, 1):
                piece = buf[h, pl.ds(8 * side(k) + 2 * b, 2)].reshape(128, 512)
                acc -= 2.0 * lax.dot_general(
                    data_ref[:, 512 * h:512 * (h + 1)], piece, (((1,), (1,)), ((), ())), preferred_element_type=F32
                )
                wide = piece.astype(F32)
                sq = wide * wide
                hi = sq.astype(BF16)
                lo = (sq - hi.astype(F32)).astype(BF16)
                for v in (hi, lo):
                    nsq += lax.dot_general(ones, v, (((1,), (1,)), ((), ())), preferred_element_type=F32)
            part[side(k), b] = (acc + nsq[0:1, :]) * scale
            return carry

        lax.fori_loop(0, 4, block, 0)

    def core_sum(k):
        return remote(part.at[side(k), :, pl.ds(128 * (1 - c), 128)], half.at[k], c_send.at[k], c_recv.at[k], other)

    def core_done(k):
        core_sum(k).wait()
        half[k] = half[k] + part[side(k), :, pl.ds(pl.multiple_of(128 * c, 128), 128)]

    def x_sum(k, i, slot):
        return remote(
            half.at[k, :, pl.ds(32 * xq(i), 32)], xin.at[k, slot], x_send.at[k, i], x_recv.at[k, slot], xpeers[i - 1]
        )

    def x_start(k):
        for i in (1, 2, 3):
            x_sum(k, i, x).start()

    def x_done(k):
        acc = half[k, :, pl.ds(pl.multiple_of(32 * x, 32), 32)]
        for i in (1, 2, 3):
            x_sum(k, i, xq(i)).wait()
            acc += xin[k, xq(i)]
        own[k] = acc

    def z_sum(k):
        return remote(own.at[k], zin.at[k], z_send.at[k], z_recv.at[k], far)

    def slab(k, cc, xx):
        return s_ref.at[pl.ds(4 * side(k), 4), pl.ds(128 * cc + 32 * xx, 32)]

    def z_done(k):
        z_sum(k).wait()
        s_ref[pl.ds(4 * side(k), 4), pl.ds(pl.multiple_of(128 * c + 32 * x, 32), 32)] = own[k] + zin[k]
        for i in (1, 2, 3):
            remote(slab(k, c, x), slab(k, c, x), gx_send.at[k, i], gx_recv.at[k, x], xpeers[i - 1]).start()

    def core_slab(k, cc):
        return s_ref.at[pl.ds(4 * side(k), 4), pl.ds(128 * cc, 128)]

    def core_gather(k, cc):
        return remote(core_slab(k, cc), core_slab(k, cc), gc_send.at[k], gc_recv.at[k], other)

    def gx_done(k):
        for i in (1, 2, 3):
            remote(slab(k, c, x), slab(k, c, xq(i)), gx_send.at[k, i], gx_recv.at[k, xq(i)], xpeers[i - 1]).wait()
        core_gather(k, c).start()

    def gc_done(k):
        core_gather(k, c).wait_send()
        core_gather(k, 1 - c).wait_recv()

    srcc = y // 2

    def spread(act):
        for h in (0, 1):
            for cc in (0, 1):
                same = jnp.logical_and(c == cc, y == 2 * c + h)
                src = data_ref.at[:, pl.ds(512 * h, 512)]

                @pl.when(jnp.logical_not(same))
                def _():
                    peer = (zh * 8 + x * 2 + cc, zl * 4 + 2 * c + h)
                    act(remote(src, dt_ref.at[y], as_.at[h, cc], ar.at[y], peer), False)

                @pl.when(same)
                def _():
                    act(pltpu.make_async_copy(src, dt_ref.at[y], loc), True)

    lax.fori_loop(0, 8 + LAG, tick, 0)
    last_column(0)
    costs(0)
    core_sum(0).start()
    lax.fori_loop(8 + LAG, 12 + LAG, tick, 0)
    core_done(0)
    x_start(0)
    lax.fori_loop(12 + LAG, 16 + LAG, tick, 0)
    last_column(1)
    costs(1)
    core_sum(1).start()
    x_done(0)
    z_sum(0).start()
    core_done(1)
    x_start(1)
    spread(lambda cp, local: cp.start())
    x_done(1)
    z_sum(1).start()
    z_done(0)
    gx_done(0)
    z_done(1)
    gx_done(1)
    gc_done(0)
    gc_done(1)

    gpot[...] = jnp.zeros_like(gpot)

    def lse0(v):
        m = jnp.max(v, axis=0)
        return m + jnp.log2(jnp.sum(jnp.exp2(v - m[None]), axis=0))

    def z_rows(k):
        for i, peer in enumerate(zpeers):
            remote(row.at[k], rz.at[k, zl], zs.at[k, i], zr.at[k, zl], peer).start()
        rz[k, zl] = row[k]

    def all_rows(k):
        for i, peer in enumerate(zpeers):
            remote(row.at[k], rz.at[k, zq(i + 1)], zs.at[k, i], zr.at[k, zq(i + 1)], peer).wait()
        ry[k, y] = lse0(rz[k])
        mine = ry.at[k, y]
        for i, peer in enumerate(ypeers):
            remote(mine, mine, ys.at[k, i], yr.at[k, y], peer).start()
        for i, peer in enumerate(ypeers):
            remote(mine, ry.at[k, yq(i + 1)], ys.at[k, i], yr.at[k, yq(i + 1)], peer).wait()
        return lse0(ry[k])

    def iteration(k, carry):
        g = gpot[...]
        for b in range(8):
            v = g - s_ref[b]
            m = jnp.max(v, axis=0, keepdims=True)
            row[k, b:b + 1, :] = m + jnp.log2(jnp.sum(jnp.exp2(v - m), axis=0, keepdims=True))
        z_rows(k)
        f = -all_rows(k)
        m = f[0:1] - s_ref[0]
        for b in range(1, 8):
            m = jnp.maximum(m, f[b:b + 1] - s_ref[b])
        m = jnp.broadcast_to(jnp.max(m, axis=1, keepdims=True), (256, 128))
        tot = jnp.zeros((256, 128), F32)
        for b in range(8):
            tot += jnp.exp2(f[b:b + 1] - s_ref[b] - m)
        tot = jnp.broadcast_to(jnp.sum(tot, axis=1, keepdims=True), (256, 128))
        gpot[...] = -(m + jnp.log2(tot))
        return carry

    lax.fori_loop(0, ITERS, iteration, 0)

    g = gpot[...]
    for b in range(8):
        v = g - s_ref[b]
        m = jnp.max(v, axis=0, keepdims=True)
        e = jnp.exp2(v - m)
        w_ref[b] = e.astype(BF16)
        mloc[b:b + 1, :] = m
        row[ITERS, b:b + 1, :] = m + jnp.log2(jnp.sum(e, axis=0, keepdims=True))

    def wsend(b, k, peer):
        return remote(w_ref.at[4 * c + b], wbuf.at[y, b], ws.at[k, b], wr.at[y, b], peer)

    def wpass(b, src, k, peer):
        return remote(wbuf.at[src, b], wbuf.at[src, b], ws.at[k, b], wr.at[src, b], peer)

    def wwait(b, src):
        remote(w_ref.at[b], wbuf.at[src, b], ws.at[0, b], wr.at[src, b], yup).wait_recv()

    left, right, opposite = yq(3), yq(1), yq(2)
    z_rows(ITERS)
    for i, peer in enumerate(ypeers):
        remote(mloc, mbuf.at[y], ms.at[i], mr.at[y], peer).start()
    for b in range(4):
        wsend(b, 0, yup).start()
        wsend(b, 1, ydown).start()
    wbuf[y] = w_ref[pl.ds(4 * c, 4)]
    mbuf[y] = mloc[...]
    for b in range(4):
        if b % 2 == 0:
            wwait(b, left)
            wpass(b, left, 2, yup).start()
        else:
            wwait(b, right)
            wpass(b, right, 2, ydown).start()
    for i, peer in enumerate(ypeers):
        remote(mloc, mbuf.at[yq(i + 1)], ms.at[i], mr.at[yq(i + 1)], peer).wait()
    lse = all_rows(ITERS)
    spread(lambda cp, local: cp.wait() if local else cp.wait_send())
    for k in range(4):
        @pl.when(jnp.logical_not(jnp.logical_and(srcc == c, y == k)))
        def _():
            peer = (zh * 8 + x * 2 + srcc, zl * 4 + k)
            remote(dt_ref.at[k], dt_ref.at[k], as_.at[0, 0], ar.at[k], peer).wait_recv()
    factor = [jnp.transpose(jnp.exp2(mbuf[k] - lse)) for k in range(4)]

    def quad(i):
        return (n, (4 * zg + (zi + i) % 4) * 4 + y)

    def quad_sum(h, i, slot):
        return remote(stage.at[h, (zi + i) % 4], qin.at[h, slot], qs.at[h, i], qr.at[h, slot], quad(i))

    for h in (0, 1):
        for bb in (0, 1):
            b = 2 * h + bb
            if b % 2 == 0:
                wwait(b, right)
            else:
                wwait(b, left)
            wwait(b, opposite)
            acc = jnp.zeros((128, 512), F32)
            for k in range(4):
                fk = jnp.where(c == 0, factor[k][:, b:b + 1], factor[k][:, 4 + b:5 + b])
                acc += fk * lax.dot_general(
                    wbuf[k, b], dt_ref[k], (((0,), (0,)), ((), ())), preferred_element_type=F32
                )
            tpart[h, 2 * bb:2 * bb + 2] = acc.reshape(2, 64, 512)
            stage[h, 2 * bb:2 * bb + 2] = acc.reshape(2, 64, 512).astype(BF16)
        for i in (1, 2, 3):
            quad_sum(h, i, zi).start()

    def final(h):
        return remote(fin.at[h], got.at[zg], fs.at[h], fr.at[zg], final_to[h])

    for h in (0, 1):
        acc = tpart[h, zi]
        for i in (1, 2, 3):
            quad_sum(h, i, (zi + i) % 4).wait()
            acc += qin[h, (zi + i) % 4].astype(F32)
        fin[h] = acc.astype(BF16)

        @pl.when(jnp.logical_not(is_me(final_to[h])))
        def _():
            final(h).start()

        @pl.when(is_me(final_to[h]))
        def _():
            pltpu.make_async_copy(fin.at[h], got.at[zg], fr.at[zg]).start()

    for g in (0, 1):
        @pl.when(jnp.logical_not(is_me(heads[g])))
        def _():
            first(g).wait_send()

    def drain(q, carry):
        for h in (0, 1):
            forwards(h, q, lambda cp: cp.wait_send())
        return carry

    lax.fori_loop(0, 16, drain, 0)
    for b in range(4):
        wsend(b, 0, yup).wait_send()
        wsend(b, 1, ydown).wait_send()
        if b % 2 == 0:
            wpass(b, left, 2, yup).wait_send()
        else:
            wpass(b, right, 2, ydown).wait_send()
    for g in (0, 1):
        pltpu.make_async_copy(fin.at[0], got.at[g], fr.at[g]).wait()
    out_ref[...] = got[0].astype(F32) + got[1].astype(F32)
    for h in (0, 1):
        @pl.when(jnp.logical_not(is_me(final_to[h])))
        def _():
            final(h).wait_send()


DMA = pltpu.SemaphoreType.DMA


def fused_call(noise, data):
    scale = LOG2E / (16384.0 * EPS)
    rounds = ITERS + 1
    return pl.pallas_call(
        functools.partial(fused_kernel, scale),
        out_shape=jax.ShapeDtypeStruct((64, 512), F32),
        in_specs=[pl.BlockSpec(memory_space=pl.ANY)] * 2,
        out_specs=pl.BlockSpec(memory_space=VMEM),
        scratch_shapes=[
            VMEM((64, 512), BF16), VMEM((256, 1024), BF16), VMEM((256, 128), F32),
            VMEM((2, 16, 64, 512), BF16),
            VMEM((2, 4, 256, 128), F32), VMEM((2, 4, 128, 128), F32), VMEM((2, 4, 4, 32, 128), F32),
            VMEM((2, 4, 32, 128), F32), VMEM((2, 4, 32, 128), F32), VMEM((8, 256, 128), F32),
            VMEM((256, 128), F32), VMEM((rounds, 8, 128), F32), VMEM((rounds, 8, 8, 128), F32),
            VMEM((rounds, 4, 8, 128), F32), VMEM((8, 128), F32),
            VMEM((8, 256, 128), BF16), VMEM((4, 256, 512), BF16), VMEM((4, 4, 256, 128), BF16),
            VMEM((4, 8, 128), F32),
            VMEM((2, 4, 64, 512), F32), VMEM((2, 4, 64, 512), BF16), VMEM((2, 4, 64, 512), BF16),
            VMEM((2, 64, 512), BF16), VMEM((2, 64, 512), BF16),
            DMA((2,)), DMA((2,)), DMA((2, 16)), DMA((2, 16, 3)),
            DMA((2,)), DMA((2,)), DMA((2, 4)), DMA((2, 4)), DMA((2,)), DMA((2,)),
            DMA((2, 4)), DMA((2, 4)), DMA((2,)), DMA((2,)),
            DMA((rounds, 7)), DMA((rounds, 8)), DMA((rounds, 3)), DMA((rounds, 4)),
            DMA((2, 2)), DMA((4,)), DMA, DMA((3, 4)), DMA((4, 4)), DMA((3,)), DMA((4,)),
            DMA((2, 4)), DMA((2, 4)), DMA((2,)), DMA((2,)),
        ],
        compiler_params=pltpu.CompilerParams(
            collective_id=1, has_side_effects=True, vmem_limit_bytes=40 * 1024 * 1024
        ),
    )(noise, data)


def per_device(noise, data, timestep):
    targets = fused_call(noise, data)
    noise_f = noise.astype(F32)
    t_val = (timestep.astype(F32) + 0.5) / NBINS
    inputs_t = ((1.0 - t_val)[:, None] * noise_f + t_val[:, None] * targets).astype(BF16)
    velocity = (targets - noise_f).astype(BF16)
    return (inputs_t, velocity)


def solution(mesh):
    placed = (P("noise", "dp"), P("dp", "noise"), P("noise"))
    return jax.shard_map(
        per_device,
        mesh=mesh,
        in_specs=placed,
        out_specs=(P("noise", "dp"), P("noise", "dp")),
        check_vma=False,
    )
```

time: 2310 us -> 156 us (0.07)
  blocking collectives: 1630 us -> 0 us
  waiting for transfers between devices: 652 us -> 0 us
  Pallas kernels: 0 us -> 152 us
    pmax x9 -> x0, blocking collectives: 813 us -> none  [the longest x5 573 us: row_lse(): peak = lax.pmax(local_peak, 'dp')]
    psum x9 -> x0, blocking collectives: 813 us -> none  [the longest x5 565 us: row_lse(): total = lax.psum(jnp.sum(jnp.exp(scores - peak[:, None]), axis=1), 'dp')]
    all_gather x2 -> x0, waiting for transfers between devices: 407 us -> none  [the longest x1 230 us: per_device(): piece = lax.all_gather(noise, 'dp', axis=1, tiled=True)]
    reduce_scatter x1 -> x0, waiting for transfers between devices: 244 us -> none  [per_device(): lax.psum_scatter(lax.dot_general(data_full, weights, (((0,), (1,)), ((),...]
    pallas_call x0 -> x1, Pallas kernels: none -> 152 us  [fused_call(): pl.pallas_call(functools.partial(fused_kernel, scale), out_shape=jax.Shap...]
  transfers between devices with their start and end apart: 3 -> 0, of which waited for: 3 -> 0; matrix products, arithmetic and copies ran while one was open for 0% -> 0% of each run, Pallas kernels for 0% -> 0%
where the time goes in v2:
time: 156 us
  Pallas kernels  152 us (97%)
  local copies, waits for them, and re-layouts  1.88 us (1%)
    pallas_call x1, Pallas kernels, fused_call(): pl.pallas_call(functools.partial(fused_kernel, scale), out_shape=jax.Shap...  152 us

profile of v2, /device:TPU:6, one launch (start us, length us, event | category | flops | bytes accessed | tf_op | source)
XLA Modules:
  0.0 155.5 jit_solution(3738180490069281410)
XLA Ops:
  0.6 0.7 broadcast_subtract_fusion
  1.3 0.0 copy-start
  1.3 1.0 copy-done
  2.3 0.0 copy-start.1
  2.3 0.8 copy-done.1
  3.2 151.6 %shard_map.50 = f32[64,512]{1,0:T(8,128)S(1)} custom-call(bf16[64,512]{1,0:T(8,128)(2,1)S(1)} %copy-done.1, bf16[256,1024]{1,0:T(8,128)(2,1)S(1)} %copy-done), custom_call_target="tpu_custom_call" | custom-call | tf_op jit(solution)/shard_map/pallas_call | solution.py:457
  154.8 0.7 fusion.2
Async XLA Ops:
  1.3 1.0 copy-start
  2.3 0.8 copy-start.1

commit v3 on v2

v3 whole, which is shorter than its diff:
```python
import functools

import jax
import jax.numpy as jnp
from jax import lax
from jax.experimental import pallas as pl
from jax.experimental.pallas import tpu as pltpu
from jax.sharding import PartitionSpec as P

ITERS = 4
NBINS = 1000
EPS = 0.002
LOG2E = 1.4426950408889634
MESH = pl.DeviceIdType.MESH
VMEM = pltpu.VMEM
F32 = jnp.float32
BF16 = jnp.bfloat16
LAG = 4
DIRECT = (False, False)


def remote(src, dst, send, recv, peer):
    return pltpu.make_async_remote_copy(
        src_ref=src, dst_ref=dst, send_sem=send, recv_sem=recv, device_id=peer, device_id_type=MESH
    )


def b2i(cond):
    return jnp.where(cond, 1, 0).astype(jnp.int32)


def fused_kernel(scale, noise_hbm, data_hbm, step_ref, out_ref, time_ref,
                 noise_ref, data_ref, dsq_ref, buf, part, half, xin, own, zin, s_ref,
                 gpot, fpot, row, rz, ry, w_ref, dt_ref, wbuf, tpart, stage, qin, fin, got,
                 load_sem, first_send, arrive, send,
                 c_send, c_recv, x_send, x_recv, z_send, z_recv, gx_send, gx_recv, gc_send, gc_recv,
                 zs, zr, ys, yr, as_, ar, loc, ws, wr, qs, qr, fs, fr):
    n, d = lax.axis_index("noise"), lax.axis_index("dp")
    zh, x, c, zl, y = n // 8, (n // 2) % 4, n % 2, d // 4, d % 4
    load_noise = pltpu.make_async_copy(noise_hbm, noise_ref, load_sem.at[0])
    load_data = pltpu.make_async_copy(data_hbm, data_ref, load_sem.at[1])
    load_noise.start()
    load_data.start()

    other_n = n + 1 - 2 * c
    other = (other_n, d)
    far = (lax.rem(n + 8, 16), d)

    def xq(k):
        return lax.rem(x + k, 4)

    def yq(k):
        return lax.rem(y + k, 4)

    def zq(k):
        return lax.rem(zl + k, 8)

    xpeers = [(zh * 8 + xq(k) * 2 + c, d) for k in (1, 2, 3)]
    ypeers = [(n, zl * 4 + yq(k)) for k in (1, 2, 3)]
    zpeers = [(n, zq(k) * 4 + y) for k in range(1, 8)]
    yup, ydown = ypeers[0], ypeers[2]
    across = [(other_n, zl * 4 + yq(k)) for k in (1, 2, 3)]
    zup, zdown = zpeers[0], zpeers[6]
    zi, zg = zl % 4, zl // 4

    head_n, head_h = d // 2, y % 2
    heads = [(head_n, (4 * g + 1 + c) * 4 + y) for g in (0, 1)]
    q_me = c * 8 + zh * 4 + x

    def is_me(peer):
        return jnp.logical_and(peer[0] == n, peer[1] == d)

    barrier = pltpu.get_barrier_semaphore()

    def greet(peer):
        pl.semaphore_signal(barrier, inc=1, device_id=peer, device_id_type=MESH)

    sym = [other, far] + xpeers + ypeers + zpeers + across
    for peer in sym:
        greet(peer)
    is_head = jnp.logical_and(c == y // 2, jnp.logical_or(zi == 1, zi == 2))

    @pl.when(is_head)
    def _():
        for k in range(8):
            peer = (k * 2 + zi // 2, (4 * zh + x) * 4 + y)

            @pl.when(jnp.logical_not(is_me(peer)))
            def _():
                greet(peer)

    final_from = [((zl // 4) * 8 + zi * 2 + c, (x + 4 * g) * 4 + y) for g in (0, 1)]
    final_to = [(h * 8 + zi * 2 + c, (4 * zh + x) * 4 + y) for h in (0, 1)]
    count = len(sym)
    for peer in final_from:
        @pl.when(jnp.logical_not(is_me(peer)))
        def _():
            greet(peer)
    for peer in heads + final_to:
        count = count + 1 - b2i(is_me(peer))
    time_ref[...] = jnp.broadcast_to(
        jnp.transpose((jnp.broadcast_to(step_ref[...], (8, 64)).astype(F32) + 0.5) / NBINS)[:, 0:1], (64, 512)
    )
    load_noise.wait()
    pl.semaphore_wait(barrier, count)

    def first(g):
        return remote(noise_ref, buf.at[head_h, q_me], first_send.at[g], arrive.at[head_h, q_me], heads[g])

    for g in (0, 1):
        @pl.when(jnp.logical_not(is_me(heads[g])))
        def _():
            first(g).start()

        @pl.when(is_me(heads[g]))
        def _():
            pltpu.make_async_copy(noise_ref, buf.at[head_h, q_me], arrive.at[head_h, q_me]).start()

    load_data.wait()
    dsq_ref[...] = jnp.broadcast_to(
        jnp.sum(jnp.square(data_ref[...].astype(F32)), axis=1, keepdims=True), (256, 128)
    )

    def landed(h, q):
        pltpu.make_async_copy(noise_ref, buf.at[h, q], arrive.at[h, q]).wait()

    def hop(h, q, kind, peer):
        return remote(buf.at[h, q], buf.at[h, q], send.at[h, q, kind], arrive.at[h, q], peer)

    near = zi // 2

    def side(k):
        return near if k == 0 else 1 - near

    def around(h):
        return lax.rem(y - (2 * c + h) + 4, 4)

    def forwards(h, q, act):
        r = around(h)
        j, upward = q % 8, q < 8
        on_chain = r == 0

        inner = jnp.logical_or(zi == 1, zi == 2)

        @pl.when(on_chain & jnp.where(upward, inner, zi == 2))
        def _():
            act(hop(h, q, 0, zup))

        @pl.when(on_chain & jnp.where(upward, zi == 1, inner))
        def _():
            act(hop(h, q, 4, zdown))

        straight = jnp.where(upward == (near == 0), DIRECT[0], DIRECT[1])
        relay = jnp.logical_not(straight)

        @pl.when(jnp.logical_or(on_chain, jnp.logical_and(relay, jnp.logical_and(r == 1, j % 2 == 0))))
        def _():
            act(hop(h, q, 1, yup))

        @pl.when(jnp.logical_or(on_chain, jnp.logical_and(relay, jnp.logical_and(r == 3, j % 2 == 1))))
        def _():
            act(hop(h, q, 2, ydown))

        @pl.when(jnp.logical_and(on_chain, straight))
        def _():
            act(hop(h, q, 3, ypeers[1]))

    def waits_early(r, k):
        return jnp.logical_and(jnp.logical_or(r == 1, r == 3), not DIRECT[k])

    def tick(t, carry):
        for lagging in (0, 1):
            for h in (0, 1):
                r = around(h)
                s = t - LAG * lagging
                mine = r == 0
                if lagging == 1:
                    mine = jnp.logical_and(waits_early(r, 0), s < 8) | jnp.logical_and(waits_early(r, 1), s >= 8)

                @pl.when(jnp.logical_and(mine, jnp.logical_and(s >= 0, s < 16)))
                def _():
                    q = 8 * jnp.where(s < 8, near, 1 - near) + s % 8
                    landed(h, q)
                    forwards(h, q, lambda cp: cp.start())
        return carry

    def last_columns(k, lo, hi):
        def body(j, carry):
            for h in (0, 1):
                r = around(h)

                @pl.when(jnp.logical_not(jnp.logical_or(r == 0, waits_early(r, k))))
                def _():
                    landed(h, 8 * side(k) + j)
            return carry

        lax.fori_loop(lo, hi, body, 0)


    blocks = (4, 2, 2)
    offset = (0, 4, 6)
    base = (4 * near, 4 - 4 * near, 6 - 4 * near)

    def costs(k):
        def pair(b, carry):
            at = base[k] + 2 * b
            acc = jnp.concatenate([dsq_ref[...]] * 2, axis=1)
            sq = jnp.zeros((256, 128), F32)
            for h in (0, 1):
                piece = buf[h, pl.ds(2 * at, 4)].reshape(256, 512)
                acc -= 2.0 * lax.dot_general(
                    data_ref[:, 512 * h:512 * (h + 1)], piece, (((1,), (1,)), ((), ())), preferred_element_type=F32
                )
                for i in range(4):
                    wide = piece[:, 128 * i:128 * (i + 1)].astype(F32)
                    sq += wide * wide
            nsq = jnp.sum(jnp.transpose(sq), axis=0, keepdims=True)
            acc = (acc + nsq) * scale
            part[offset[k] + 2 * b] = acc[:, 0:128]
            part[offset[k] + 2 * b + 1] = acc[:, 128:256]
            return carry

        lax.fori_loop(0, blocks[k] // 2, pair, 0)

    def chunk(k):
        return pl.ds(offset[k], blocks[k])

    def core_sum(k):
        return remote(
            part.at[chunk(k), pl.ds(128 * (1 - c), 128)], half.at[chunk(k)], c_send.at[k], c_recv.at[k], other
        )

    def core_done(k):
        core_sum(k).wait()
        half[chunk(k)] = half[chunk(k)] + part[chunk(k), pl.ds(pl.multiple_of(128 * c, 128), 128)]

    def x_sum(k, i, slot):
        return remote(
            half.at[chunk(k), pl.ds(32 * xq(i), 32)], xin.at[slot, chunk(k)],
            x_send.at[k, i], x_recv.at[k, slot], xpeers[i - 1],
        )

    def x_start(k):
        for i in (1, 2, 3):
            x_sum(k, i, x).start()

    def z_sum(k):
        return remote(own.at[chunk(k)], zin.at[chunk(k)], z_send.at[k], z_recv.at[k], far)

    def x_done(k):
        acc = half[chunk(k), pl.ds(pl.multiple_of(32 * x, 32), 32)]
        for i in (1, 2, 3):
            x_sum(k, i, xq(i)).wait()
            acc += xin[xq(i), chunk(k)]
        own[chunk(k)] = acc
        z_sum(k).start()

    def slab(k, cc, xx):
        return s_ref.at[pl.ds(base[k], blocks[k]), pl.ds(128 * cc + 32 * xx, 32)]

    def z_done(k):
        z_sum(k).wait()
        mine = pl.ds(pl.multiple_of(128 * c + 32 * x, 32), 32)
        s_ref[pl.ds(base[k], blocks[k]), mine] = own[chunk(k)] + zin[chunk(k)]
        for i in (1, 2, 3):
            remote(slab(k, c, x), slab(k, c, x), gx_send.at[k, i], gx_recv.at[k, x], xpeers[i - 1]).start()

    def core_gather(k, cc):
        place = s_ref.at[pl.ds(base[k], blocks[k]), pl.ds(128 * cc, 128)]
        return remote(place, place, gc_send.at[k], gc_recv.at[k], other)

    def gx_done(k):
        for i in (1, 2, 3):
            remote(slab(k, c, x), slab(k, c, xq(i)), gx_send.at[k, i], gx_recv.at[k, xq(i)], xpeers[i - 1]).wait()
        core_gather(k, c).start()

    def gc_done(k):
        core_gather(k, c).wait_send()
        core_gather(k, 1 - c).wait_recv()

    srcc = y // 2

    def spread(act):
        for h in (0, 1):
            for cc in (0, 1):
                same = jnp.logical_and(c == cc, y == 2 * c + h)
                src = data_ref.at[:, pl.ds(512 * h, 512)]

                @pl.when(jnp.logical_not(same))
                def _():
                    peer = (zh * 8 + x * 2 + cc, zl * 4 + 2 * c + h)
                    act(remote(src, dt_ref.at[y], as_.at[h, cc], ar.at[y], peer), False)

                @pl.when(same)
                def _():
                    act(pltpu.make_async_copy(src, dt_ref.at[y], loc), True)

    lax.fori_loop(0, 8 + LAG, tick, 0)
    last_columns(0, 0, 8)
    costs(0)
    core_sum(0).start()
    lax.fori_loop(8 + LAG, 12 + LAG, tick, 0)
    core_done(0)
    x_start(0)
    last_columns(1, 0, 4)
    costs(1)
    core_sum(1).start()
    lax.fori_loop(12 + LAG, 16 + LAG, tick, 0)
    x_done(0)
    core_done(1)
    x_start(1)
    last_columns(1, 4, 8)
    costs(2)
    core_sum(2).start()
    x_done(1)
    core_done(2)
    x_start(2)
    spread(lambda cp, local: cp.start())
    x_done(2)
    z_done(0)
    gx_done(0)
    z_done(1)
    gx_done(1)
    z_done(2)
    gx_done(2)
    for k in range(3):
        gc_done(k)

    def lse0(v):
        m = jnp.max(v, axis=0)
        return m + jnp.log2(jnp.sum(jnp.exp2(v - m[None]), axis=0))

    def z_rows(k):
        for i, peer in enumerate(zpeers):
            remote(row.at[k], rz.at[k, zl], zs.at[k, i], zr.at[k, zl], peer).start()
        rz[k, zl] = row[k]

    def all_rows(k, total):
        for i, peer in enumerate(zpeers):
            remote(row.at[k], rz.at[k, zq(i + 1)], zs.at[k, i], zr.at[k, zq(i + 1)], peer).wait()
        ry[k, y] = total(rz[k])
        mine = ry.at[k, y]
        for i, peer in enumerate(ypeers):
            remote(mine, mine, ys.at[k, i], yr.at[k, y], peer).start()
        for i, peer in enumerate(ypeers):
            remote(mine, ry.at[k, yq(i + 1)], ys.at[k, i], yr.at[k, yq(i + 1)], peer).wait()
        return total(ry[k])

    for b in range(8):
        v = -s_ref[b]
        m = jnp.max(v, axis=0, keepdims=True)
        row[0, b:b + 1, :] = m + jnp.log2(jnp.sum(jnp.exp2(v - m), axis=0, keepdims=True))
    z_rows(0)
    f = -all_rows(0, lse0)
    fpot[...] = f
    m = f[0:1] - s_ref[0]
    for b in range(1, 8):
        m = jnp.maximum(m, f[b:b + 1] - s_ref[b])
    m = jnp.broadcast_to(jnp.max(m, axis=1, keepdims=True), (256, 128))
    tot = jnp.zeros((256, 128), F32)
    for b in range(8):
        tot += jnp.exp2(f[b:b + 1] - s_ref[b] - m)
    gpot[...] = -(m + jnp.log2(jnp.broadcast_to(jnp.sum(tot, axis=1, keepdims=True), (256, 128))))

    def add0(v):
        return jnp.sum(v, axis=0)

    def iteration(k, carry):
        g = gpot[...]
        f = fpot[...]
        for b in range(8):
            row[k, b:b + 1, :] = jnp.sum(jnp.exp2(g - s_ref[b] + f[b:b + 1]), axis=0, keepdims=True)
        z_rows(k)
        f = f - jnp.log2(all_rows(k, add0))
        fpot[...] = f
        tot = jnp.zeros((256, 128), F32)
        for b in range(8):
            tot += jnp.exp2(g - s_ref[b] + f[b:b + 1])
        gpot[...] = g - jnp.log2(jnp.broadcast_to(jnp.sum(tot, axis=1, keepdims=True), (256, 128)))
        return carry

    lax.fori_loop(1, ITERS, iteration, 0)

    g = gpot[...]
    f = fpot[...]
    for b in (0, 1, 4, 5, 2, 3, 6, 7):
        e = jnp.exp2(g - s_ref[b] + f[b:b + 1])
        w_ref[b] = e.astype(BF16)
        row[ITERS, b:b + 1, :] = jnp.sum(e, axis=0, keepdims=True)

    def wsend(b, k, peer):
        return remote(w_ref.at[4 * c + b], wbuf.at[y, b], ws.at[k, b], wr.at[y, b], peer)

    def wpass(b, src, k, peer):
        return remote(wbuf.at[src, b], wbuf.at[src, b], ws.at[k, b], wr.at[src, b], peer)

    def wwait(b, src):
        remote(w_ref.at[b], wbuf.at[src, b], ws.at[0, b], wr.at[src, b], yup).wait_recv()

    left, right, opposite = yq(3), yq(1), yq(2)
    for b in range(4):
        wsend(b, 0, yup).start()
        wsend(b, 1, ydown).start()
    z_rows(ITERS)
    wbuf[y] = w_ref[pl.ds(4 * c, 4)]
    spread(lambda cp, local: cp.wait() if local else cp.wait_send())
    for k in range(4):
        @pl.when(jnp.logical_not(jnp.logical_and(srcc == c, y == k)))
        def _():
            peer = (zh * 8 + x * 2 + srcc, zl * 4 + k)
            remote(dt_ref.at[k], dt_ref.at[k], as_.at[0, 0], ar.at[k], peer).wait_recv()

    def wforward(b):
        if b % 2 == 0:
            wwait(b, left)
            wpass(b, left, 2, yup).start()
        else:
            wwait(b, right)
            wpass(b, right, 2, ydown).start()

    def quad(i):
        return (n, (4 * zg + (zi + i) % 4) * 4 + y)

    def quad_sum(h, i, slot):
        return remote(stage.at[h, (zi + i) % 4], qin.at[h, slot], qs.at[h, i], qr.at[h, slot], quad(i))

    wforward(0)
    wforward(1)
    for h in (0, 1):
        for bb in (0, 1):
            b = 2 * h + bb
            wwait(b, right if b % 2 == 0 else left)
            wwait(b, opposite)
            acc = jnp.zeros((128, 512), F32)
            for k in range(4):
                acc += lax.dot_general(
                    wbuf[k, b], dt_ref[k], (((0,), (0,)), ((), ())), preferred_element_type=F32
                )
            tpart[h, 2 * bb:2 * bb + 2] = acc.reshape(2, 64, 512)
            stage[h, 2 * bb:2 * bb + 2] = acc.reshape(2, 64, 512).astype(BF16)
        for i in (1, 2, 3):
            quad_sum(h, i, zi).start()
        if h == 0:
            wforward(2)
            wforward(3)

    def final(h):
        return remote(fin.at[h], got.at[zg], fs.at[h], fr.at[zg], final_to[h])

    for h in (0, 1):
        acc = tpart[h, zi]
        for i in (1, 2, 3):
            quad_sum(h, i, (zi + i) % 4).wait()
            acc += qin[h, (zi + i) % 4].astype(F32)
        fin[h] = acc.astype(BF16)

        @pl.when(jnp.logical_not(is_me(final_to[h])))
        def _():
            final(h).start()

        @pl.when(is_me(final_to[h]))
        def _():
            pltpu.make_async_copy(fin.at[h], got.at[zg], fr.at[zg]).start()

    total = 1.0 / all_rows(ITERS, add0)
    columns = jnp.transpose(total)
    mine_b = 4 * c + 2 * zh + x // 2
    picked = jnp.zeros((128, 1), F32)
    for b in range(8):
        picked = jnp.where(mine_b == b, columns[:, b:b + 1], picked)
    picked = jnp.where(x % 2 == 0, picked[0:64], picked[64:128])

    for g in (0, 1):
        @pl.when(jnp.logical_not(is_me(heads[g])))
        def _():
            first(g).wait_send()

    def drain(q, carry):
        for h in (0, 1):
            forwards(h, q, lambda cp: cp.wait_send())
        return carry

    lax.fori_loop(0, 16, drain, 0)
    for b in range(4):
        wsend(b, 0, yup).wait_send()
        wsend(b, 1, ydown).wait_send()
        if b % 2 == 0:
            wpass(b, left, 2, yup).wait_send()
        else:
            wpass(b, right, 2, ydown).wait_send()
    for g in (0, 1):
        pltpu.make_async_copy(fin.at[0], got.at[g], fr.at[g]).wait()
    out_ref[...] = (got[0].astype(F32) + got[1].astype(F32)) * picked
    for h in (0, 1):
        @pl.when(jnp.logical_not(is_me(final_to[h])))
        def _():
            final(h).wait_send()


DMA = pltpu.SemaphoreType.DMA


def fused_call(noise, data, timestep):
    scale = LOG2E / (16384.0 * EPS)
    rounds = ITERS + 1
    return pl.pallas_call(
        functools.partial(fused_kernel, scale),
        out_shape=[jax.ShapeDtypeStruct((64, 512), F32), jax.ShapeDtypeStruct((64, 512), F32)],
        in_specs=[pl.BlockSpec(memory_space=pl.ANY)] * 2 + [pl.BlockSpec(memory_space=VMEM)],
        out_specs=[pl.BlockSpec(memory_space=VMEM)] * 2,
        scratch_shapes=[
            VMEM((64, 512), BF16), VMEM((256, 1024), BF16), VMEM((256, 128), F32),
            VMEM((2, 16, 64, 512), BF16),
            VMEM((8, 256, 128), F32), VMEM((8, 128, 128), F32), VMEM((4, 8, 32, 128), F32),
            VMEM((8, 32, 128), F32), VMEM((8, 32, 128), F32), VMEM((8, 256, 128), F32),
            VMEM((256, 128), F32), VMEM((8, 128), F32), VMEM((rounds, 8, 128), F32), VMEM((rounds, 8, 8, 128), F32),
            VMEM((rounds, 4, 8, 128), F32),
            VMEM((8, 256, 128), BF16), VMEM((4, 256, 512), BF16), VMEM((4, 4, 256, 128), BF16),
            VMEM((2, 4, 64, 512), F32), VMEM((2, 4, 64, 512), BF16), VMEM((2, 4, 64, 512), BF16),
            VMEM((2, 64, 512), BF16), VMEM((2, 64, 512), BF16),
            DMA((2,)), DMA((2,)), DMA((2, 16)), DMA((2, 16, 5)),
            DMA((3,)), DMA((3,)), DMA((3, 4)), DMA((3, 4)), DMA((3,)), DMA((3,)),
            DMA((3, 4)), DMA((3, 4)), DMA((3,)), DMA((3,)),
            DMA((rounds, 7)), DMA((rounds, 8)), DMA((rounds, 3)), DMA((rounds, 4)),
            DMA((2, 2)), DMA((4,)), DMA, DMA((3, 4)), DMA((4, 4)),
            DMA((2, 4)), DMA((2, 4)), DMA((2,)), DMA((2,)),
        ],
        compiler_params=pltpu.CompilerParams(
            collective_id=1, has_side_effects=True, vmem_limit_bytes=62 * 1024 * 1024
        ),
    )(noise, data, timestep)


def per_device(noise, data, timestep):
    targets, t_wide = fused_call(noise, data, timestep.reshape(1, 64))
    noise_f = noise.astype(F32)
    t_val = t_wide
    inputs_t = ((1.0 - t_val) * noise_f + t_val * targets).astype(BF16)
    velocity = (targets - noise_f).astype(BF16)
    return (inputs_t, velocity)


def solution(mesh):
    placed = (P("noise", "dp"), P("dp", "noise"), P("noise"))
    return jax.shard_map(
        per_device,
        mesh=mesh,
        in_specs=placed,
        out_specs=(P("noise", "dp"), P("noise", "dp")),
        check_vma=False,
    )
```

time: 156 us -> 151 us (0.968)
  Pallas kernels: 152 us -> 147 us
  local copies, waits for them, and re-layouts: 1.88 us -> 0.01 us
    pallas_call x1, Pallas kernels: 152 us -> 147 us  [fused_call(): pl.pallas_call(functools.partial(fused_kernel, scale), out_shape=[jax.Sha...]
    unnamed x4 -> x2, local copies, waits for them, and re-layouts: 1.88 us -> 0.01 us
where the time goes in v3:
time: 151 us; the launch traced here: 149 us
  Pallas kernels  147 us (97%)
  other arithmetic  1.65 us (1%)
    pallas_call x1, Pallas kernels, fused_call(): pl.pallas_call(functools.partial(fused_kernel, scale), out_shape=[jax.Sha...  147 us

profile of v3, /device:TPU:6, one launch (start us, length us, event | category | flops | bytes accessed | tf_op | source)
XLA Modules:
  0.0 149.0 jit_solution(15994871246848024899)
XLA Ops:
  0.6 0.0 copy-start
  0.6 146.7 %shard_map.50 = (f32[64,512]{1,0:T(8,128)}, f32[64,512]{1,0:T(8,128)}) custom-call(bf16[64,512]{1,0:T(8,128)(2,1)} %noise_hbm.1, bf16[256,1024]{1,0:T(8,128)(2,1)} %data_hbm.1, s32[1,64]{1,0:T(1,128)} %bitcast.1), custom_call_target="tpu_custom_call" | custom-call | tf_op jit(solution)/shard_map/pallas_call | solution.py:506
  147.4 0.0 copy-done
  147.4 1.7 %fusion.2 = (bf16[64,512]{1,0:T(8,128)(2,1)}, bf16[64,512]{1,0:T(8,128)(2,1)}) fusion(f32[64,512]{1,0:T(8,128)} %get-tuple-element.5, bf16[64,512]{1,0:T(8,128)(2,1)S(1)} %copy-done, f32[64,512]{1,0:T(8,128)} %get-tuple-element.4), kind=kLoop, calls=%fused_computation.4 | loop fusion | flops 262144 | bytes 458752 | tf_op jit(solution)/shard_map/convert_element_type | solution.py:539
Async XLA Ops:
  0.6 146.7 %copy-start = (bf16[64,512]{1,0:T(8,128)(2,1)S(1)}, bf16[64,512]{1,0:T(8,128)(2,1)}, u32[]{:S(2)}) copy-start(bf16[64,512]{1,0:T(8,128)(2,1)} %noise_hbm.1) | copy-start | bytes 196612

commit v4 on v3

--- a/solution.py
+++ b/solution.py
@@ -16,7 +16,7 @@
 F32 = jnp.float32
 BF16 = jnp.bfloat16
 LAG = 4
-DIRECT = (False, False)
+DIRECT = (True, False)
 
 
 def remote(src, dst, send, recv, peer):
@@ -31,10 +31,10 @@
 
 def fused_kernel(scale, noise_hbm, data_hbm, step_ref, out_ref, time_ref,
                  noise_ref, data_ref, dsq_ref, buf, part, half, xin, own, zin, s_ref,
-                 gpot, fpot, row, rz, ry, w_ref, dt_ref, wbuf, tpart, stage, qin, fin, got,
+                 gpot, fpot, pin, cin, row, rz, ry, w_ref, dt_ref, wbuf, tpart, stage, qin, fin, got,
                  load_sem, first_send, arrive, send,
                  c_send, c_recv, x_send, x_recv, z_send, z_recv, gx_send, gx_recv, gc_send, gc_recv,
-                 zs, zr, ys, yr, as_, ar, loc, ws, wr, qs, qr, fs, fr):
+                 ps, pr, cs, cr, zs, zr, ys, yr, as_, ar, loc, ws, wr, qs, qr, fs, fr):
     n, d = lax.axis_index("noise"), lax.axis_index("dp")
     zh, x, c, zl, y = n // 8, (n // 2) % 4, n % 2, d // 4, d % 4
     load_noise = pltpu.make_async_copy(noise_hbm, noise_ref, load_sem.at[0])
@@ -61,6 +61,9 @@
     yup, ydown = ypeers[0], ypeers[2]
     across = [(other_n, zl * 4 + yq(k)) for k in (1, 2, 3)]
     zup, zdown = zpeers[0], zpeers[6]
+    shifts = [(i, j) for i in range(4) for j in range(4) if i + j > 0]
+    plane = [(zh * 8 + xq(i) * 2 + c, zl * 4 + yq(j)) for i, j in shifts]
+    corners = [peer for peer, (i, j) in zip(plane, shifts) if i > 0 and j > 0]
     zi, zg = zl % 4, zl // 4
 
     head_n, head_h = d // 2, y % 2
@@ -75,7 +78,7 @@
     def greet(peer):
         pl.semaphore_signal(barrier, inc=1, device_id=peer, device_id_type=MESH)
 
-    sym = [other, far] + xpeers + ypeers + zpeers + across
+    sym = [other, far] + xpeers + ypeers + zpeers + across + corners
     for peer in sym:
         greet(peer)
     is_head = jnp.logical_and(c == y // 2, jnp.logical_or(zi == 1, zi == 2))
@@ -321,11 +324,6 @@
     gx_done(0)
     z_done(1)
     gx_done(1)
-    z_done(2)
-    gx_done(2)
-    for k in range(3):
-        gc_done(k)
-
     def lse0(v):
         m = jnp.max(v, axis=0)
         return m + jnp.log2(jnp.sum(jnp.exp2(v - m[None]), axis=0))
@@ -334,6 +332,15 @@
         for i, peer in enumerate(zpeers):
             remote(row.at[k], rz.at[k, zl], zs.at[k, i], zr.at[k, zl], peer).start()
         rz[k, zl] = row[k]
+
+    z_done(2)
+    v = -s_ref[:, pl.ds(pl.multiple_of(128 * c + 32 * x, 32), 32)]
+    m = jnp.max(v, axis=1)
+    row[0] = m + jnp.log2(jnp.sum(jnp.exp2(v - m[:, None]), axis=1))
+    z_rows(0)
+    gx_done(2)
+    for k in range(3):
+        gc_done(k)
 
     def all_rows(k, total):
         for i, peer in enumerate(zpeers):
@@ -346,12 +353,19 @@
             remote(mine, ry.at[k, yq(i + 1)], ys.at[k, i], yr.at[k, yq(i + 1)], peer).wait()
         return total(ry[k])
 
-    for b in range(8):
-        v = -s_ref[b]
-        m = jnp.max(v, axis=0, keepdims=True)
-        row[0, b:b + 1, :] = m + jnp.log2(jnp.sum(jnp.exp2(v - m), axis=0, keepdims=True))
-    z_rows(0)
-    f = -all_rows(0, lse0)
+    for i, peer in enumerate(zpeers):
+        remote(row.at[0], rz.at[0, zq(i + 1)], zs.at[0, i], zr.at[0, zq(i + 1)], peer).wait()
+    spot = 4 * x + y
+    pin[spot] = lse0(rz[0])
+    for i, peer in enumerate(plane):
+        remote(pin.at[spot], pin.at[spot], ps.at[i], pr.at[spot], peer).start()
+    for i, peer in enumerate(plane):
+        there = 4 * xq(shifts[i][0]) + yq(shifts[i][1])
+        remote(pin.at[spot], pin.at[there], ps.at[i], pr.at[there], peer).wait()
+    cin[c] = lse0(pin[...])
+    remote(cin.at[c], cin.at[c], cs.at[0], cr.at[c], other).start()
+    remote(cin.at[c], cin.at[1 - c], cs.at[0], cr.at[1 - c], other).wait()
+    f = -lse0(cin[...])
     fpot[...] = f
     m = f[0:1] - s_ref[0]
     for b in range(1, 8):
@@ -381,13 +395,6 @@
 
     lax.fori_loop(1, ITERS, iteration, 0)
 
-    g = gpot[...]
-    f = fpot[...]
-    for b in (0, 1, 4, 5, 2, 3, 6, 7):
-        e = jnp.exp2(g - s_ref[b] + f[b:b + 1])
-        w_ref[b] = e.astype(BF16)
-        row[ITERS, b:b + 1, :] = jnp.sum(e, axis=0, keepdims=True)
-
     def wsend(b, k, peer):
         return remote(w_ref.at[4 * c + b], wbuf.at[y, b], ws.at[k, b], wr.at[y, b], peer)
 
@@ -398,11 +405,16 @@
         remote(w_ref.at[b], wbuf.at[src, b], ws.at[0, b], wr.at[src, b], yup).wait_recv()
 
     left, right, opposite = yq(3), yq(1), yq(2)
+    g = gpot[...]
+    row[ITERS] = jnp.zeros((8, 128), F32)
     for b in range(4):
+        e = jnp.exp2(g - s_ref[4 * c + b] + fpot[pl.ds(4 * c + b, 1), :])
+        w_ref[4 * c + b] = e.astype(BF16)
         wsend(b, 0, yup).start()
         wsend(b, 1, ydown).start()
+        wbuf[y, b] = e.astype(BF16)
+        row[ITERS, b:b + 1, :] = jnp.sum(e, axis=0, keepdims=True)
     z_rows(ITERS)
-    wbuf[y] = w_ref[pl.ds(4 * c, 4)]
     spread(lambda cp, local: cp.wait() if local else cp.wait_send())
     for k in range(4):
         @pl.when(jnp.logical_not(jnp.logical_and(srcc == c, y == k)))
@@ -424,25 +436,53 @@
     def quad_sum(h, i, slot):
         return remote(stage.at[h, (zi + i) % 4], qin.at[h, slot], qs.at[h, i], qr.at[h, slot], quad(i))
 
+    def mul(b, k):
+        prod = lax.dot_general(wbuf[k, b], dt_ref[k], (((0,), (0,)), ((), ())), preferred_element_type=F32)
+        return prod.reshape(2, 64, 512)
+
+    def place(b):
+        return b // 2, pl.ds(2 * (b % 2), 2)
+
+    def add(b, k):
+        h, at = place(b)
+        tpart[h, at] += mul(b, k)
+
+    def finish(b):
+        wwait(b, opposite)
+        h, at = place(b)
+        acc = tpart[h, at] + mul(b, opposite)
+        tpart[h, at] = acc
+        stage[h, at] = acc.astype(BF16)
+
+    def quad_start(h):
+        for i in (1, 2, 3):
+            quad_sum(h, i, zi).start()
+
+    for b in range(4):
+        h, at = place(b)
+        tpart[h, at] = mul(b, y)
     wforward(0)
     wforward(1)
-    for h in (0, 1):
-        for bb in (0, 1):
-            b = 2 * h + bb
-            wwait(b, right if b % 2 == 0 else left)
-            wwait(b, opposite)
-            acc = jnp.zeros((128, 512), F32)
-            for k in range(4):
-                acc += lax.dot_general(
-                    wbuf[k, b], dt_ref[k], (((0,), (0,)), ((), ())), preferred_element_type=F32
-                )
-            tpart[h, 2 * bb:2 * bb + 2] = acc.reshape(2, 64, 512)
-            stage[h, 2 * bb:2 * bb + 2] = acc.reshape(2, 64, 512).astype(BF16)
-        for i in (1, 2, 3):
-            quad_sum(h, i, zi).start()
-        if h == 0:
-            wforward(2)
-            wforward(3)
+    add(0, left)
+    add(1, right)
+    wforward(2)
+    wforward(3)
+    wwait(0, right)
+    add(0, right)
+    wwait(1, left)
+    add(1, left)
+    finish(0)
+    finish(1)
+    quad_start(0)
+    add(2, left)
+    add(3, right)
+    wwait(2, right)
+    add(2, right)
+    wwait(3, left)
+    add(3, left)
+    finish(2)
+    finish(3)
+    quad_start(1)
 
     def final(h):
         return remote(fin.at[h], got.at[zg], fs.at[h], fr.at[zg], final_to[h])
@@ -464,9 +504,9 @@
 
     total = 1.0 / all_rows(ITERS, add0)
     columns = jnp.transpose(total)
-    mine_b = 4 * c + 2 * zh + x // 2
+    mine_b = 2 * zh + x // 2
     picked = jnp.zeros((128, 1), F32)
-    for b in range(8):
+    for b in range(4):
         picked = jnp.where(mine_b == b, columns[:, b:b + 1], picked)
     picked = jnp.where(x % 2 == 0, picked[0:64], picked[64:128])
 
@@ -513,7 +553,7 @@
             VMEM((2, 16, 64, 512), BF16),
             VMEM((8, 256, 128), F32), VMEM((8, 128, 128), F32), VMEM((4, 8, 32, 128), F32),
             VMEM((8, 32, 128), F32), VMEM((8, 32, 128), F32), VMEM((8, 256, 128), F32),
-            VMEM((256, 128), F32), VMEM((8, 128), F32), VMEM((rounds, 8, 128), F32), VMEM((rounds, 8, 8, 128), F32),
+            VMEM((256, 128), F32), VMEM((8, 128), F32), VMEM((16, 8, 128), F32), VMEM((2, 8, 128), F32), VMEM((rounds, 8, 128), F32), VMEM((rounds, 8, 8, 128), F32),
             VMEM((rounds, 4, 8, 128), F32),
             VMEM((8, 256, 128), BF16), VMEM((4, 256, 512), BF16), VMEM((4, 4, 256, 128), BF16),
             VMEM((2, 4, 64, 512), F32), VMEM((2, 4, 64, 512), BF16), VMEM((2, 4, 64, 512), BF16),
@@ -521,12 +561,13 @@
             DMA((2,)), DMA((2,)), DMA((2, 16)), DMA((2, 16, 5)),
             DMA((3,)), DMA((3,)), DMA((3, 4)), DMA((3, 4)), DMA((3,)), DMA((3,)),
             DMA((3, 4)), DMA((3, 4)), DMA((3,)), DMA((3,)),
+            DMA((15,)), DMA((16,)), DMA((1,)), DMA((2,)),
             DMA((rounds, 7)), DMA((rounds, 8)), DMA((rounds, 3)), DMA((rounds, 4)),
             DMA((2, 2)), DMA((4,)), DMA, DMA((3, 4)), DMA((4, 4)),
             DMA((2, 4)), DMA((2, 4)), DMA((2,)), DMA((2,)),
         ],
         compiler_params=pltpu.CompilerParams(
-            collective_id=1, has_side_effects=True, vmem_limit_bytes=62 * 1024 * 1024
+            collective_id=1, has_side_effects=True, vmem_limit_bytes=40 * 1024 * 1024
         ),
     )(noise, data, timestep)
 

time: 151 us -> 152 us (level)
  the two profiles are of different devices: /device:TPU:6 before, /device:TPU:2 now
where the time goes in v4:
time: 152 us
  Pallas kernels  148 us (97%)
  local copies, waits for them, and re-layouts  2.53 us (2%)
    pallas_call x1, Pallas kernels, fused_call(): pl.pallas_call(functools.partial(fused_kernel, scale), out_shape=[jax.Sha...  148 us

profile of v4, /device:TPU:2, one launch (start us, length us, event | category | flops | bytes accessed | tf_op | source)
XLA Modules:
  0.0 152.1 jit_solution(3677838669189119865)
XLA Ops:
  0.6 0.0 copy-start.2
  0.6 0.6 copy-done.2
  1.3 0.0 copy-start
  1.3 1.0 copy-done
  2.3 0.0 copy-start.1
  2.3 0.8 copy-done.1
  3.2 148.3 %shard_map.50 = (f32[64,512]{1,0:T(8,128)S(1)}, f32[64,512]{1,0:T(8,128)S(1)}) custom-call(bf16[64,512]{1,0:T(8,128)(2,1)S(1)} %copy-done.1, bf16[256,1024]{1,0:T(8,128)(2,1)S(1)} %copy-done, s32[1,64]{1,0:T(1,128)S(1)} %bitcast.1), custom_call_target="tpu_custom_call" | custom-call | tf_op jit(solution)/shard_map/pallas_call | solution.py:546
  151.5 0.7 fusion.2
Async XLA Ops:
  0.6 0.7 copy-start.2
  1.3 1.0 copy-start
  2.3 0.8 copy-start.1

commit v5 on v4

--- a/solution.py
+++ b/solution.py
@@ -16,7 +16,7 @@
 F32 = jnp.float32
 BF16 = jnp.bfloat16
 LAG = 4
-DIRECT = (True, False)
+DIRECT = (False, False)
 
 
 def remote(src, dst, send, recv, peer):
@@ -31,10 +31,10 @@
 
 def fused_kernel(scale, noise_hbm, data_hbm, step_ref, out_ref, time_ref,
                  noise_ref, data_ref, dsq_ref, buf, part, half, xin, own, zin, s_ref,
-                 gpot, fpot, pin, cin, row, rz, ry, w_ref, dt_ref, wbuf, tpart, stage, qin, fin, got,
+                 gpot, fpot, row, rz, ry, w_ref, dt_ref, wbuf, tpart, stage, qin, fin, got,
                  load_sem, first_send, arrive, send,
                  c_send, c_recv, x_send, x_recv, z_send, z_recv, gx_send, gx_recv, gc_send, gc_recv,
-                 ps, pr, cs, cr, zs, zr, ys, yr, as_, ar, loc, ws, wr, qs, qr, fs, fr):
+                 zs, zr, ys, yr, as_, ar, loc, ws, wr, qs, qr, fs, fr):
     n, d = lax.axis_index("noise"), lax.axis_index("dp")
     zh, x, c, zl, y = n // 8, (n // 2) % 4, n % 2, d // 4, d % 4
     load_noise = pltpu.make_async_copy(noise_hbm, noise_ref, load_sem.at[0])
@@ -61,9 +61,6 @@
     yup, ydown = ypeers[0], ypeers[2]
     across = [(other_n, zl * 4 + yq(k)) for k in (1, 2, 3)]
     zup, zdown = zpeers[0], zpeers[6]
-    shifts = [(i, j) for i in range(4) for j in range(4) if i + j > 0]
-    plane = [(zh * 8 + xq(i) * 2 + c, zl * 4 + yq(j)) for i, j in shifts]
-    corners = [peer for peer, (i, j) in zip(plane, shifts) if i > 0 and j > 0]
     zi, zg = zl % 4, zl // 4
 
     head_n, head_h = d // 2, y % 2
@@ -78,7 +75,7 @@
     def greet(peer):
         pl.semaphore_signal(barrier, inc=1, device_id=peer, device_id_type=MESH)
 
-    sym = [other, far] + xpeers + ypeers + zpeers + across + corners
+    sym = [other, far] + xpeers + ypeers + zpeers + across
     for peer in sym:
         greet(peer)
     is_head = jnp.logical_and(c == y // 2, jnp.logical_or(zi == 1, zi == 2))
@@ -324,6 +321,11 @@
     gx_done(0)
     z_done(1)
     gx_done(1)
+    z_done(2)
+    gx_done(2)
+    for k in range(3):
+        gc_done(k)
+
     def lse0(v):
         m = jnp.max(v, axis=0)
         return m + jnp.log2(jnp.sum(jnp.exp2(v - m[None]), axis=0))
@@ -332,15 +334,6 @@
         for i, peer in enumerate(zpeers):
             remote(row.at[k], rz.at[k, zl], zs.at[k, i], zr.at[k, zl], peer).start()
         rz[k, zl] = row[k]
-
-    z_done(2)
-    v = -s_ref[:, pl.ds(pl.multiple_of(128 * c + 32 * x, 32), 32)]
-    m = jnp.max(v, axis=1)
-    row[0] = m + jnp.log2(jnp.sum(jnp.exp2(v - m[:, None]), axis=1))
-    z_rows(0)
-    gx_done(2)
-    for k in range(3):
-        gc_done(k)
 
     def all_rows(k, total):
         for i, peer in enumerate(zpeers):
@@ -353,19 +346,12 @@
             remote(mine, ry.at[k, yq(i + 1)], ys.at[k, i], yr.at[k, yq(i + 1)], peer).wait()
         return total(ry[k])
 
-    for i, peer in enumerate(zpeers):
-        remote(row.at[0], rz.at[0, zq(i + 1)], zs.at[0, i], zr.at[0, zq(i + 1)], peer).wait()
-    spot = 4 * x + y
-    pin[spot] = lse0(rz[0])
-    for i, peer in enumerate(plane):
-        remote(pin.at[spot], pin.at[spot], ps.at[i], pr.at[spot], peer).start()
-    for i, peer in enumerate(plane):
-        there = 4 * xq(shifts[i][0]) + yq(shifts[i][1])
-        remote(pin.at[spot], pin.at[there], ps.at[i], pr.at[there], peer).wait()
-    cin[c] = lse0(pin[...])
-    remote(cin.at[c], cin.at[c], cs.at[0], cr.at[c], other).start()
-    remote(cin.at[c], cin.at[1 - c], cs.at[0], cr.at[1 - c], other).wait()
-    f = -lse0(cin[...])
+    for b in range(8):
+        v = -s_ref[b]
+        m = jnp.max(v, axis=0, keepdims=True)
+        row[0, b:b + 1, :] = m + jnp.log2(jnp.sum(jnp.exp2(v - m), axis=0, keepdims=True))
+    z_rows(0)
+    f = -all_rows(0, lse0)
     fpot[...] = f
     m = f[0:1] - s_ref[0]
     for b in range(1, 8):
@@ -553,7 +539,7 @@
             VMEM((2, 16, 64, 512), BF16),
             VMEM((8, 256, 128), F32), VMEM((8, 128, 128), F32), VMEM((4, 8, 32, 128), F32),
             VMEM((8, 32, 128), F32), VMEM((8, 32, 128), F32), VMEM((8, 256, 128), F32),
-            VMEM((256, 128), F32), VMEM((8, 128), F32), VMEM((16, 8, 128), F32), VMEM((2, 8, 128), F32), VMEM((rounds, 8, 128), F32), VMEM((rounds, 8, 8, 128), F32),
+            VMEM((256, 128), F32), VMEM((8, 128), F32), VMEM((rounds, 8, 128), F32), VMEM((rounds, 8, 8, 128), F32),
             VMEM((rounds, 4, 8, 128), F32),
             VMEM((8, 256, 128), BF16), VMEM((4, 256, 512), BF16), VMEM((4, 4, 256, 128), BF16),
             VMEM((2, 4, 64, 512), F32), VMEM((2, 4, 64, 512), BF16), VMEM((2, 4, 64, 512), BF16),
@@ -561,13 +547,12 @@
             DMA((2,)), DMA((2,)), DMA((2, 16)), DMA((2, 16, 5)),
             DMA((3,)), DMA((3,)), DMA((3, 4)), DMA((3, 4)), DMA((3,)), DMA((3,)),
             DMA((3, 4)), DMA((3, 4)), DMA((3,)), DMA((3,)),
-            DMA((15,)), DMA((16,)), DMA((1,)), DMA((2,)),
             DMA((rounds, 7)), DMA((rounds, 8)), DMA((rounds, 3)), DMA((rounds, 4)),
             DMA((2, 2)), DMA((4,)), DMA, DMA((3, 4)), DMA((4, 4)),
             DMA((2, 4)), DMA((2, 4)), DMA((2,)), DMA((2,)),
         ],
         compiler_params=pltpu.CompilerParams(
-            collective_id=1, has_side_effects=True, vmem_limit_bytes=40 * 1024 * 1024
+            collective_id=1, has_side_effects=True, vmem_limit_bytes=62 * 1024 * 1024
         ),
     )(noise, data, timestep)
 

time: 152 us -> 151 us (level)
  the two profiles are of different devices: /device:TPU:2 before, /device:TPU:6 now
where the time goes in v5:
time: 151 us
  Pallas kernels  149 us (99%)
  other arithmetic  1.65 us (1%)
    pallas_call x1, Pallas kernels, fused_call(): pl.pallas_call(functools.partial(fused_kernel, scale), out_shape=[jax.Sha...  149 us

profile of v5, /device:TPU:6, one launch (start us, length us, event | category | flops | bytes accessed | tf_op | source)
XLA Modules:
  0.0 150.9 jit_solution(15640005631116729934)
XLA Ops:
  0.6 0.0 copy-start
  0.6 148.6 %shard_map.50 = (f32[64,512]{1,0:T(8,128)}, f32[64,512]{1,0:T(8,128)}) custom-call(bf16[64,512]{1,0:T(8,128)(2,1)} %noise_hbm.1, bf16[256,1024]{1,0:T(8,128)(2,1)} %data_hbm.1, s32[1,64]{1,0:T(1,128)} %bitcast.1), custom_call_target="tpu_custom_call" | custom-call | tf_op jit(solution)/shard_map/pallas_call | solution.py:532
  149.3 0.0 copy-done
  149.3 1.7 %fusion.2 = (bf16[64,512]{1,0:T(8,128)(2,1)}, bf16[64,512]{1,0:T(8,128)(2,1)}) fusion(f32[64,512]{1,0:T(8,128)} %get-tuple-element.5, bf16[64,512]{1,0:T(8,128)(2,1)S(1)} %copy-done, f32[64,512]{1,0:T(8,128)} %get-tuple-element.4), kind=kLoop, calls=%fused_computation.4 | loop fusion | flops 262144 | bytes 458752 | tf_op jit(solution)/shard_map/convert_element_type | solution.py:565
Async XLA Ops:
  0.6 148.6 %copy-start = (bf16[64,512]{1,0:T(8,128)(2,1)S(1)}, bf16[64,512]{1,0:T(8,128)(2,1)}, u32[]{:S(2)}) copy-start(bf16[64,512]{1,0:T(8,128)(2,1)} %noise_hbm.1) | copy-start | bytes 196612
